TPU v7x, 512 devices: a whole 4x4x16 slice. The times are simulated.
512 devices in a mesh: rep: 8 (over z_lo, core), fsdp: 64 (over y, x, z_hi).
Axes of the slice: x: 4, y: 4, z: 16 (z_hi: 4, z_lo: 4; z = z_hi * 4 + z_lo), core: 2. Of those that a mesh axis runs over, the one named last changes fastest.
Arguments:
- tokens: bfloat16 [4096, 4096], P('rep', 'fsdp'), may hold values from -6 to 6
- norm_gain: bfloat16 [4096], replicated, may hold values from 0.099609375 to 1.8984375
- gate_weight: bfloat16 [8, 5632, 4096], P('rep', 'fsdp'), may hold values from -0.09375 to 0.09375
- up_weight: bfloat16 [8, 5632, 4096], P('rep', 'fsdp'), may hold values from -0.09375 to 0.09375
- down_weight: bfloat16 [8, 5632, 4096], P('rep', 'fsdp'), may hold values from -0.09375 to 0.09375
- cotangent: bfloat16 [4096, 4096], P('rep', 'fsdp'), may hold values from -6 to 6
- outer_delta: bfloat16 [8, 5632, 4096], P('rep', 'fsdp'), may hold values from -6 to 6
- momentum: float32 [5632, 4096], P(('fsdp', 'rep')), may hold values from -6 to 6
- anchor: bfloat16 [5632, 4096], P(('fsdp', 'rep')), may hold values from -6 to 6
Outputs:
- gate_grad: bfloat16 [8, 5632, 4096], P('rep', 'fsdp')
- up_grad: bfloat16 [8, 5632, 4096], P('rep', 'fsdp')
- new_momentum: float32 [5632, 4096], P(('fsdp', 'rep'))
- new_anchor: bfloat16 [5632, 4096], P(('fsdp', 'rep'))
All inputs are finite; a program needn't handle non-finite values.
Results may differ from a plain program's by a relative error of at most 0.009.
Values may be sent and summed in bfloat16 or wider, within the bound.
A program may use at most 64 MiB of HBM per device.

v0:
```python
import jax
import jax.numpy as jnp
from jax import lax
from jax.sharding import PartitionSpec as P

norm_epsilon = 1e-06
outer_beta = 0.9
outer_rate = 0.7


def body(
    tokens, norm_gain, gate_weight, up_weight, down_weight, cotangent, outer_delta, momentum, anchor
):
    gate_rows = gate_weight[0]
    up_rows = up_weight[0]
    down_rows = down_weight[0]
    contract = (((1,), (1,)), ((), ()))
    all_tokens, all_upstream = (
        lax.all_gather(tokens, "fsdp", axis=1, tiled=True),
        lax.all_gather(cotangent, "fsdp", axis=1, tiled=True),
    )
    values = all_tokens.astype(jnp.float32)
    scale = jnp.sqrt(jnp.mean(values * values, axis=1, keepdims=True) + norm_epsilon)
    normed = (values / scale * norm_gain.astype(jnp.float32)).astype(jnp.bfloat16)
    gate_pre = lax.dot_general(normed, gate_rows, contract, preferred_element_type=jnp.float32)
    up_pre = lax.dot_general(normed, up_rows, contract, preferred_element_type=jnp.float32)
    back = lax.dot_general(all_upstream, down_rows, contract, preferred_element_type=jnp.float32)
    sig = jax.nn.sigmoid(gate_pre)
    d_gate = (back * up_pre * sig * (1.0 + gate_pre * (1.0 - sig))).astype(jnp.bfloat16)
    d_up = (back * gate_pre * sig).astype(jnp.bfloat16)
    tokens_dim = (((0,), (0,)), ((), ()))
    grad_gate = lax.dot_general(d_gate, normed, tokens_dim, preferred_element_type=jnp.float32)
    grad_up = lax.dot_general(d_up, normed, tokens_dim, preferred_element_type=jnp.float32)
    replicas = lax.axis_size("rep")
    delta = outer_delta[0].astype(jnp.float32)
    total = lax.psum(delta.astype(jnp.bfloat16), "rep").astype(jnp.float32)
    share = anchor.shape[0]
    mine = lax.dynamic_slice_in_dim(total, lax.axis_index("rep") * share, share, 0)
    mean_delta = mine / replicas
    new_momentum = outer_beta * momentum + mean_delta
    new_anchor = (
        anchor.astype(jnp.float32) - outer_rate * (mean_delta + outer_beta * new_momentum)
    ).astype(jnp.bfloat16)
    return (
        grad_gate.astype(jnp.bfloat16)[None],
        grad_up.astype(jnp.bfloat16)[None],
        new_momentum,
        new_anchor,
    )


def solution(mesh):
    return jax.shard_map(
        body,
        mesh=mesh,
        in_specs=(
            P("rep", "fsdp"),
            P(),
            P("rep", "fsdp", None),
            P("rep", "fsdp", None),
            P("rep", "fsdp", None),
            P("rep", "fsdp"),
            P("rep", "fsdp", None),
            P(("fsdp", "rep"), None),
            P(("fsdp", "rep"), None),
        ),
        out_specs=(
            P("rep", "fsdp", None),
            P("rep", "fsdp", None),
            P(("fsdp", "rep"), None),
            P(("fsdp", "rep"), None),
        ),
        check_vma=False,
    )
```

profile of v0, /device:TPU:6, one launch (start us, length us, event | category | flops | bytes accessed | tf_op | source)
XLA Modules:
  0.0 318.0 jit_solution(12603907047271641428)
XLA Ops:
  8.0 0.0 copy-start
  8.0 0.0 all-reduce.2.cloned.1.call-start
  8.1 0.7 all-reduce.2.cloned.1.call-update
  8.7 0.0 all-gather.5.cloned.1.call-start
  8.8 0.5 all-gather.5.cloned.1.call-update
  9.3 0.0 all-gather.3.cloned.1.call-start
  9.4 0.5 all-gather.3.cloned.1.call-update
  9.9 0.7 convert_element_type.33
  10.6 90.4 %all-reduce.2.cloned.1.call-done = bf16[88,4096]{1,0:T(8,128)(2,1)} async-done(((bf16[88,4096]{1,0:T(8,128)(2,1)}), bf16[88,4096]{1,0:T(8,128)(2,1)}) %all-reduce.2.cloned.1.call-update) | async-done | bytes 720912 | tf_op jit(solution)/shard_map/psum | solution.py:36
  101.0 2.0 subtract_convert_fusion
  103.0 55.7 %all-gather.5.cloned.1.call-done = bf16[512,4096]{0,1:T(8,128)(2,1)} async-done(((bf16[512,64]{0,1:T(8,128)(2,1)}), bf16[512,4096]{0,1:T(8,128)(2,1)}) %all-gather.5.cloned.1.call-update) | async-done | bytes 4194320 | tf_op jit(solution)/shard_map/all_gather | solution.py:19
  158.7 0.0 copy-start.3
  158.7 3.3 %fusion = f32[512]{0:T(512)S(1)} fusion(bf16[512,4096]{0,1:T(8,128)(2,1)} %all-gather.5.cloned.1.call-done), kind=kLoop, calls=%fused_computation.2 | loop fusion | flops 6290944 | bytes 4196352 | tf_op jit(solution)/shard_map/reduce_sum | solution.py:23
  162.0 0.2 copy-done.3
  162.1 0.0 copy-start.4
  162.1 1.1 fusion.2
  163.2 0.0 copy-start.1
  163.2 2.0 copy-done.1
  165.2 0.0 copy-done.4
  165.2 0.0 copy-start.5
  165.2 0.8 fusion.8
  166.0 132.4 %all-gather.3.cloned.1.call-done = bf16[512,4096]{0,1:T(8,128)(2,1)} async-done(((bf16[512,64]{0,1:T(8,128)(2,1)}), bf16[512,4096]{0,1:T(8,128)(2,1)}) %all-gather.3.cloned.1.call-update) | async-done | bytes 4194320 | tf_op jit(solution)/shard_map/all_gather | solution.py:20
  298.4 0.0 copy-done.5
  298.4 0.0 copy-start.2
  298.4 3.2 fusion.12
  301.6 0.3 copy-done.2
  301.8 2.3 fusion.4
  304.1 0.0 copy-done
  304.1 6.5 %fusion.3 = bf16[1,88,4096]{2,1,0:T(8,128)(2,1)} fusion(bf16[512,4096]{0,1:T(8,128)(2,1)} %copy-done.1, f32[512,88]{0,1:T(8,128)S(1)} %fusion.12, bf16[1,88,4096]{2,1,0:T(8,128)(2,1)S(1)} %copy-done, f32[512,88]{0,1:T(8,128)S(1)} %fusion.8), kind=kOutput, calls=%fused_computation.7 | convolution fusion | flops 739008512 | bytes 5996544 | tf_op jit(solution)/shard_map/dot_general | solution.py:32
  (1 shorter events, 0.0 us)
Async XLA Ops:
  8.0 296.1 %copy-start = (bf16[1,88,4096]{2,1,0:T(8,128)(2,1)S(1)}, bf16[1,88,4096]{2,1,0:T(8,128)(2,1)}, u32[]{:S(2)}) copy-start(bf16[1,88,4096]{2,1,0:T(8,128)(2,1)} %param.12) | copy-start | bytes 2162692
  8.0 93.0 %all-reduce.2.cloned.1.call-start = ((), (), s32[]{:S(2)}) async-start(), calls=%async_computation.2 | async-start | bytes 1441792 | tf_op jit(solution)/shard_map/psum | solution.py:36
  8.7 149.9 %all-gather.5.cloned.1.call-start = ((), (), s32[]{:S(2)}) async-start(), calls=%async_computation.1 | async-start | bytes 4259840 | tf_op jit(solution)/shard_map/all_gather | solution.py:19
  9.3 289.1 %all-gather.3.cloned.1.call-start = ((), (), s32[]{:S(2)}) async-start(), calls=%async_computation | async-start | bytes 4259840 | tf_op jit(solution)/shard_map/all_gather | solution.py:20
  158.7 3.4 %copy-start.3 = (bf16[512,4096]{0,1:T(8,128)(2,1)S(1)}, bf16[512,4096]{0,1:T(8,128)(2,1)}, u32[]{:S(2)}) copy-start(bf16[512,4096]{0,1:T(8,128)(2,1)} %all-gather.5.cloned.1.call-done) | copy-start | bytes 12582916
  162.1 3.1 copy-start.4
  163.2 2.0 copy-start.1
  165.2 133.2 %copy-start.5 = (bf16[1,88,4096]{2,1,0:T(8,128)(2,1)S(1)}, bf16[1,88,4096]{2,1,0:T(8,128)(2,1)}, u32[]{:S(2)}) copy-start(bf16[1,88,4096]{2,1,0:T(8,128)(2,1)} %param.13) | copy-start | bytes 2162692
  298.4 3.4 %copy-start.2 = (bf16[512,4096]{0,1:T(8,128)(2,1)S(1)}, bf16[512,4096]{0,1:T(8,128)(2,1)}, u32[]{:S(2)}) copy-start(bf16[512,4096]{0,1:T(8,128)(2,1)} %copy-done.1) | copy-start | bytes 12582916
Sparse Core Ops, SparseCore 0:
  11.8 89.1 all-reduce.1
Sparse Core Ops, SparseCore 1:
  13.4 145.2 all-gather.4
  162.7 135.6 all-gather.2
where the time goes:
time: 319 us; the launch traced here: 318 us
  waiting for transfers between devices  280 us (88%)
  between operations  15.5 us (5%)
  matrix products  12.7 us (4%)
  other arithmetic  7.02 us (2%)
    all_gather x1, waiting for transfers between devices, body(): lax.all_gather(cotangent, 'fsdp', axis=1, tiled=True)  132 us
    psum x1, waiting for transfers between devices, body(): total = lax.psum(delta.astype(jnp.bfloat16), 'rep').astype(jnp.float32)  90.4 us
    all_gather x1, waiting for transfers between devices, body(): lax.all_gather(tokens, 'fsdp', axis=1, tiled=True)  55.7 us
    dot_general x1, matrix products, body(): lax.dot_general(d_gate, normed, tokens_dim, preferred_element_type=jnp.fl...  6.47 us
  transfers between devices with their start and end apart: 3, of which 3 were waited for; matrix products, arithmetic and copies ran while one was open for 2% of the time, Pallas kernels for 0%

commit v1 on v0

v1 whole, which is shorter than its diff:
```python
import functools

import jax
import jax.numpy as jnp
from jax import lax
from jax.experimental import pallas as pl
from jax.experimental.pallas import tpu as pltpu
from jax.sharding import PartitionSpec as P

norm_epsilon = 1e-06
outer_beta = 0.9
outer_rate = 0.7

MESH = pl.DeviceIdType.MESH
F32 = jnp.float32
BF16 = jnp.bfloat16
D = 4096
HID = 88
NT = (((1,), (1,)), ((), ()))
NN = (((1,), (0,)), ((), ()))
TOK, COT = 0, 1
GROUPS = ((0, 1), (1, 4))
TASKS = ((TOK, 0), (COT, 0), (TOK, 3), (TOK, 1), (TOK, 2), (COT, 3), (COT, 1), (COT, 2))


def kernel(
    tok_ref, cot_ref, gain_ref, gate_hbm, up_hbm, down_hbm, delta_hbm, mom_ref, anchor_ref,
    grad_gate, grad_up, new_mom, new_anchor,
    g, normed, gate_w, up_w, down_w, delta_v, gate_up, diag, acc_pre, acc_back, squares, d_t,
    share, pair_in, pair_out, line_in,
    load_sem, send, recv, zsend, zrecv, osend, orecv,
):
    f = lax.axis_index("fsdp")
    r = lax.axis_index("rep")
    y, x, zh = f // 16, (f // 4) % 4, f % 4
    zl, core = r // 2, r % 2

    def at(yy, xx, zz):
        return {"fsdp": ((yy + 4) % 4) * 16 + ((xx + 4) % 4) * 4 + (zz + 4) % 4}

    xn = (at(y, x + 1, zh), at(y, x - 1, zh))
    yn = (at(y + 1, x, zh), at(y - 1, x, zh))
    zn = (at(y, x, zh + 1), at(y, x, zh - 1))
    partner = {"rep": zl * 2 + 1 - core}
    line = [{"rep": ((zl + k) % 4) * 2 + core} for k in (1, 2, 3)]

    barrier = pltpu.get_barrier_semaphore()
    peers = [*xn, *yn, *zn, partner, *line]
    for peer in peers:
        pl.semaphore_signal(barrier, inc=1, device_id=peer, device_id_type=MESH)

    loads = [
        pltpu.make_async_copy(src, dst, load_sem.at[i])
        for i, (src, dst) in enumerate(
            ((delta_hbm, delta_v), (gate_hbm, gate_w), (up_hbm, up_w), (down_hbm, down_w))
        )
    ]
    for load in loads:
        load.start()

    def pack(t, ref):
        for h in range(2):
            top = ref[h * 256 : h * 256 + 128, :]
            bottom = ref[h * 256 + 128 : h * 256 + 256, :]
            g[t, h, 0, 0, 0] = jnp.concatenate([top, bottom], axis=1)

    pack(TOK, tok_ref)
    pack(COT, cot_ref)
    pl.semaphore_wait(barrier, len(peers))

    started, arrived = {}, set()

    def start(key, src, dst, ssem, rsem, device):
        copy = pltpu.make_async_remote_copy(
            src_ref=src, dst_ref=dst, send_sem=ssem, recv_sem=rsem,
            device_id=device, device_id_type=MESH,
        )
        copy.start()
        started[key] = copy

    def need(key):
        if key not in arrived:
            arrived.add(key)
            started[key].wait_recv()

    def xy(task, h, k, src, dst, device):
        t, rz = task
        start((task, h, k), src, dst, send.at[t, h, rz, k], recv.at[t, h, rz, k], device)

    def near(h):
        return (xn, yn) if h == 0 else (yn, xn)

    lo, hi = pl.ds(0, 64), pl.ds(64, 64)

    def first_send(task):
        for h in range(2):
            b = g.at[task[0], h, task[1]]
            xy(task, h, 0, b.at[0, 0], b.at[0, 3], near(h)[0][0])
            xy(task, h, 1, b.at[0, 0], b.at[0, 1], near(h)[0][1])

    def first_forward(task):
        for h in range(2):
            b = g.at[task[0], h, task[1]]
            need((task, h, 0))
            xy(task, h, 2, b.at[0, 3, lo], b.at[0, 2, lo], near(h)[0][0])
            need((task, h, 1))
            xy(task, h, 3, b.at[0, 1, hi], b.at[0, 2, hi], near(h)[0][1])

    def second_send(task, i):
        for h in range(2):
            b = g.at[task[0], h, task[1]]
            if i > 0:
                for k in range(4):
                    need((task, h, k))
            cols = pl.ds(GROUPS[i][0], GROUPS[i][1] - GROUPS[i][0])
            xy(task, h, 4 + 4 * i, b.at[0, cols], b.at[3, cols], near(h)[1][0])
            xy(task, h, 5 + 4 * i, b.at[0, cols], b.at[1, cols], near(h)[1][1])

    def second_forward(task, i):
        for h in range(2):
            b = g.at[task[0], h, task[1]]
            cols = pl.ds(GROUPS[i][0], GROUPS[i][1] - GROUPS[i][0])
            need((task, h, 4 + 4 * i))
            xy(task, h, 6 + 4 * i, b.at[3, cols, lo], b.at[2, cols, lo], near(h)[1][0])
            need((task, h, 5 + 4 * i))
            xy(task, h, 7 + 4 * i, b.at[1, cols, hi], b.at[2, cols, hi], near(h)[1][1])

    def z_send(t):
        for h in range(2):
            start(("z", t, h, 0), g.at[t, h, 0, 0, 0], g.at[t, h, 3, 0, 0],
                  zsend.at[t, h, 0], zrecv.at[t, h, 0], zn[0])
        for h in (1, 0):
            start(("z", t, h, 1), g.at[t, h, 0, 0, 0], g.at[t, h, 1, 0, 0],
                  zsend.at[t, h, 1], zrecv.at[t, h, 1], zn[1])

    def z_forward(t):
        need(("z", t, 0, 0))
        start(("z", t, 0, 2), g.at[t, 0, 3, 0, 0], g.at[t, 0, 2, 0, 0],
              zsend.at[t, 0, 2], zrecv.at[t, 0, 2], zn[0])
        need(("z", t, 1, 1))
        start(("z", t, 1, 2), g.at[t, 1, 1, 0, 0], g.at[t, 1, 2, 0, 0],
              zsend.at[t, 1, 2], zrecv.at[t, 1, 2], zn[1])

    def z_need(task):
        t, rz = task
        if rz:
            for h in range(2):
                need(("z", t, h, {3: 0, 1: 1, 2: 2}[rz]))

    def step_i(task):
        z_need(task)
        first_send(task)
        second_send(task, 0)

    def step_m(task):
        first_forward(task)
        second_forward(task, 0)

    def step_d(task):
        for h in range(2):
            for i in range(len(GROUPS)):
                need((task, h, 6 + 4 * i))
                need((task, h, 7 + 4 * i))

    def outer_pack():
        loads[0].wait()

        @pl.loop(0, 8)
        def _(c):
            cols = pl.ds(pl.multiple_of(c * 512, 512), 512)
            rows = delta_v[:, cols].astype(F32)
            for b in range(8):
                if b < 7:
                    block = rows[b * 11 : b * 11 + 16]
                else:
                    block = jnp.concatenate([rows[77:88], jnp.zeros((5, 512), F32)], axis=0)
                share[b % 2, b // 2, :, cols] = block.astype(BF16)

    def outer_pair():
        start("pair", share.at[1 - core], pair_in, osend.at[0], orecv.at[0], partner)

    def outer_line():
        need("pair")

        @pl.loop(0, 4)
        def _(b):
            pair_out[b] = (share[core, b].astype(F32) + pair_in[b].astype(F32)).astype(BF16)

        for k in range(3):
            start(("line", k), pair_out.at[(zl + k + 1) % 4], line_in.at[k],
                  osend.at[1 + k], orecv.at[1 + k], line[k])

    def outer_finish():
        for k in range(3):
            need(("line", k))
        total = share[core, zl].astype(F32) + pair_in[zl].astype(F32)
        for k in range(3):
            total = total + line_in[k].astype(F32)
        mean_delta = total[:11] / 8.0
        momentum = outer_beta * mom_ref[...] + mean_delta
        new_mom[...] = momentum
        new_anchor[...] = (
            anchor_ref[...].astype(F32) - outer_rate * (mean_delta + outer_beta * momentum)
        ).astype(BF16)

    low_lanes = lax.broadcasted_iota(jnp.int32, (128, 128), 1) < 64

    def prep_gate_up():
        loads[1].wait()
        loads[2].wait()

        @pl.loop(0, 8)
        def _(c):
            cols = pl.ds(pl.multiple_of(c * 512, 512), 512)
            gate_up[:, cols] = jnp.concatenate(
                [gate_w[:, cols].astype(F32), up_w[:, cols].astype(F32)], axis=0
            ).astype(BF16)

    def prep_down():
        loads[3].wait()
        low = low_lanes[:HID]

        @pl.loop(0, 16)
        def _(b):
            for pair in range(2):
                cols = pl.ds(pl.multiple_of(b * 256 + pair * 128, 128), 128)
                w = down_w[:, cols].astype(F32)
                turned = pltpu.roll(w, 64, 1)
                zero = jnp.zeros_like(w)
                diag[2 * pair, b] = jnp.concatenate(
                    [jnp.where(low, w, zero), jnp.where(low, zero, turned)], axis=0
                ).astype(BF16)
                diag[2 * pair + 1, b] = jnp.concatenate(
                    [jnp.where(low, turned, zero), jnp.where(low, zero, w)], axis=0
                ).astype(BF16)
        acc_back[...] = jnp.zeros_like(acc_back)
        acc_pre[...] = jnp.zeros_like(acc_pre)
        squares[...] = jnp.zeros_like(squares)

    def unpack(first, last):
        @pl.loop(first, last)
        def _(b):
            ry, rx = (b // 4 - y + 4) % 4, (b % 4 - x + 4) % 4
            for h in range(2):
                parts = [
                    g[TOK, h, (zs - zh + 4) % 4, ry if h == 0 else rx, rx if h == 0 else ry].astype(F32)
                    for zs in range(4)
                ]
                for pair in range(2):
                    even, odd = parts[2 * pair], parts[2 * pair + 1]
                    top = jnp.where(low_lanes, even, pltpu.roll(odd, 64, 1))
                    bottom = jnp.where(low_lanes, pltpu.roll(even, 64, 1), odd)
                    cols = pl.ds(pl.multiple_of(b * 256 + pair * 128, 128), 128)
                    for i, block in enumerate((top, bottom)):
                        rows = pl.ds(h * 256 + i * 128, 128)
                        normed[rows, cols] = block.astype(BF16)
                        squares[rows, :] += block * block

    def inverse_scale():
        total = jnp.sum(squares[...], axis=1, keepdims=True)
        squares[...] = jnp.broadcast_to(
            1.0 / jnp.sqrt(total / D + norm_epsilon), squares.shape
        )

    def forward(first, last):
        @pl.loop(first, last)
        def _(b):
            cols = pl.ds(pl.multiple_of(b * 256, 256), 256)
            gain = gain_ref[:, cols].astype(F32)
            scale = squares[...]
            scale = jnp.concatenate([scale, scale], axis=1)
            block = (normed[:, cols].astype(F32) * scale * gain).astype(BF16)
            normed[:, cols] = block
            acc_pre[...] += lax.dot_general(
                gate_up[:, cols], block, NT, preferred_element_type=F32
            )

    def backward(task):
        step_d(task)
        rz = task[1]
        zs = (zh + rz) % 4

        @pl.loop(0, 4)
        def _(ry):
            ws, rows = [], []
            for rx in range(4):
                ws.append(diag[zs, ((y + ry) % 4) * 4 + (x + rx) % 4])
            for h in range(2):
                rows.append(
                    jnp.concatenate(
                        [
                            g[COT, h, rz, ry if h == 0 else rx, rx if h == 0 else ry]
                            for rx in range(4)
                        ],
                        axis=1,
                    )
                )
            acc_back[...] += lax.dot_general(
                jnp.concatenate(ws, axis=1), jnp.concatenate(rows, axis=0), NT,
                preferred_element_type=F32,
            )

    def finish():
        for q in range(4):
            lanes = pl.ds(q * 128, 128)
            gate_pre = acc_pre[:HID, lanes]
            up_pre = acc_pre[HID:, lanes]
            half = pl.ds((q // 2) * 128, 128)
            back = acc_back[HID * (q % 2) : HID * (q % 2) + HID, half]
            sig = jax.nn.sigmoid(gate_pre)
            d_gate = back * up_pre * sig * (1.0 + gate_pre * (1.0 - sig))
            d_up = back * gate_pre * sig
            d_t[:, lanes] = jnp.concatenate([d_gate, d_up], axis=0).astype(BF16)

        @pl.loop(0, 8)
        def _(c):
            cols = pl.ds(pl.multiple_of(c * 512, 512), 512)
            out = lax.dot_general(d_t[...], normed[:, cols], NN, preferred_element_type=F32)
            grad_gate[:, cols] = out[:HID].astype(BF16)
            grad_up[:, cols] = out[HID:].astype(BF16)

    T = TASKS
    n = len(T)
    z_send(TOK)
    step_i(T[0])
    step_i(T[1])
    z_send(COT)
    outer_pack()
    outer_pair()
    step_m(T[0])
    work = {
        0: [prep_gate_up, lambda: z_forward(TOK)],
        1: [prep_down],
        2: [lambda: z_forward(COT)],
        3: [outer_line, lambda: backward(T[1])],
        6: [lambda: step_d(T[0]), lambda: step_d(T[2]), lambda: step_d(T[3]), lambda: step_d(T[4]), lambda: unpack(0, 16)],
        7: [inverse_scale, lambda: forward(0, 16), outer_finish],
        8: [lambda: backward(T[5])],
        9: [lambda: backward(T[6])],
    }
    for i in range(n + 2):
        if i < n:
            second_send(T[i], 1)
        if i + 1 < n:
            step_m(T[i + 1])
        if i + 2 < n:
            step_i(T[i + 2])
        if 0 <= i - 1 < n:
            second_forward(T[i - 1], 1)
        for piece in work.get(i, ()):
            piece()
    backward(T[7])
    for key, copy in started.items():
        if key not in arrived:
            need(key)
        copy.wait_send()
    finish()


def body(
    tokens, norm_gain, gate_weight, up_weight, down_weight, cotangent, outer_delta, momentum, anchor
):
    vmem = pl.BlockSpec(memory_space=pltpu.VMEM)
    hbm = pl.BlockSpec(memory_space=pl.ANY)
    nk = 4 + 4 * len(GROUPS)
    dma = pltpu.SemaphoreType.DMA
    outs = pl.pallas_call(
        kernel,
        out_shape=(
            jax.ShapeDtypeStruct((HID, D), BF16),
            jax.ShapeDtypeStruct((HID, D), BF16),
            jax.ShapeDtypeStruct((11, D), F32),
            jax.ShapeDtypeStruct((11, D), BF16),
        ),
        in_specs=[vmem, vmem, vmem, hbm, hbm, hbm, hbm, vmem, vmem],
        out_specs=(vmem, vmem, vmem, vmem),
        scratch_shapes=[
            pltpu.VMEM((2, 2, 4, 4, 4, 128, 128), BF16),
            pltpu.VMEM((512, D), BF16),
            pltpu.VMEM((HID, D), BF16),
            pltpu.VMEM((HID, D), BF16),
            pltpu.VMEM((HID, D), BF16),
            pltpu.VMEM((HID, D), BF16),
            pltpu.VMEM((2 * HID, D), BF16),
            pltpu.VMEM((4, 16, 2 * HID, 128), BF16),
            pltpu.VMEM((2 * HID, 512), F32),
            pltpu.VMEM((2 * HID, 256), F32),
            pltpu.VMEM((512, 128), F32),
            pltpu.VMEM((2 * HID, 512), BF16),
            pltpu.VMEM((2, 4, 16, D), BF16),
            pltpu.VMEM((4, 16, D), BF16),
            pltpu.VMEM((4, 16, D), BF16),
            pltpu.VMEM((3, 16, D), BF16),
            dma((4,)),
            dma((2, 2, 4, nk)),
            dma((2, 2, 4, nk)),
            dma((2, 2, 3)),
            dma((2, 2, 3)),
            dma((4,)),
            dma((4,)),
        ],
        compiler_params=pltpu.CompilerParams(
            collective_id=0, has_side_effects=True, vmem_limit_bytes=48 * 2**20
        ),
        cost_estimate=pl.CostEstimate(
            flops=10 * 512 * D * HID, bytes_accessed=8 * 2**20, transcendentals=512 * HID
        ),
        name="gather_and_grads",
    )(
        tokens, cotangent, norm_gain.reshape(1, D), gate_weight[0], up_weight[0], down_weight[0],
        outer_delta[0], momentum, anchor,
    )
    return outs[0][None], outs[1][None], outs[2], outs[3]


def solution(mesh):
    return jax.shard_map(
        body,
        mesh=mesh,
        in_specs=(
            P("rep", "fsdp"),
            P(),
            P("rep", "fsdp", None),
            P("rep", "fsdp", None),
            P("rep", "fsdp", None),
            P("rep", "fsdp"),
            P("rep", "fsdp", None),
            P(("fsdp", "rep"), None),
            P(("fsdp", "rep"), None),
        ),
        out_specs=(
            P("rep", "fsdp", None),
            P("rep", "fsdp", None),
            P(("fsdp", "rep"), None),
            P(("fsdp", "rep"), None),
        ),
        check_vma=False,
    )
```

time: 319 us -> 86.3 us (0.27)
  the two profiles are of different devices: /device:TPU:6 before, /device:TPU:32 now
where the time goes in v1:
time: 86.3 us; the launch traced here: 85.9 us
  Pallas kernels  75 us (87%)
  local copies, waits for them, and re-layouts  10.2 us (12%)
    pallas_call x1, Pallas kernels, body(): pl.pallas_call(kernel, out_shape=(jax.ShapeDtypeStruct((HID, D), BF16), j...  75 us
    unnamed x18, local copies, waits for them, and re-layouts  9.47 us

profile of v1, /device:TPU:32, one launch (start us, length us, event | category | flops | bytes accessed | tf_op | source)
XLA Modules:
  0.0 85.9 jit_solution(11420628298033037283)
XLA Ops:
  0.6 0.0 copy-start.4
  0.6 0.8 reshape.11.gain_ref
  1.4 1.0 %copy.13.tok_ref = bf16[512,64]{1,0:T(8,128)(2,1)S(1)} copy(bf16[512,64]{0,1:T(8,128)(2,1)} %param.9) | data formatting | bytes 131072 | tf_op args[0]
  2.4 0.0 copy-start.5
  2.4 1.0 %copy.14.cot_ref = bf16[512,64]{1,0:T(8,128)(2,1)S(1)} copy(bf16[512,64]{0,1:T(8,128)(2,1)} %param.14) | data formatting | bytes 131072 | tf_op args[5]
  3.4 0.0 copy-done.4
  3.4 0.0 copy-done.5
  3.4 0.0 copy-start
  3.4 1.1 %copy-done = bf16[1,88,4096]{2,1,0:T(8,128)(2,1)S(1)} copy-done((bf16[1,88,4096]{2,1,0:T(8,128)(2,1)S(1)}, bf16[1,88,4096]{2,1,0:T(8,128)(2,1)}, u32[]{:S(2)}) %copy-start) | copy-done | bytes 720920
  4.5 0.0 copy-start.1
  4.5 1.1 %copy-done.1 = bf16[1,88,4096]{2,1,0:T(8,128)(2,1)S(1)} copy-done((bf16[1,88,4096]{2,1,0:T(8,128)(2,1)S(1)}, bf16[1,88,4096]{2,1,0:T(8,128)(2,1)}, u32[]{:S(2)}) %copy-start.1) | copy-done | bytes 720920
  5.6 0.0 copy-start.2
  5.6 1.1 %copy-done.2 = bf16[1,88,4096]{2,1,0:T(8,128)(2,1)S(1)} copy-done((bf16[1,88,4096]{2,1,0:T(8,128)(2,1)S(1)}, bf16[1,88,4096]{2,1,0:T(8,128)(2,1)}, u32[]{:S(2)}) %copy-start.2) | copy-done | bytes 720920
  6.7 0.0 copy-start.3
  6.7 1.1 %copy-done.3 = bf16[1,88,4096]{2,1,0:T(8,128)(2,1)S(1)} copy-done((bf16[1,88,4096]{2,1,0:T(8,128)(2,1)S(1)}, bf16[1,88,4096]{2,1,0:T(8,128)(2,1)}, u32[]{:S(2)}) %copy-start.3) | copy-done | bytes 720920
  7.8 75.0 %gather_and_grads.1 = (bf16[88,4096]{1,0:T(8,128)(2,1)S(1)}, bf16[88,4096]{1,0:T(8,128)(2,1)S(1)}, f32[11,4096]{1,0:T(8,128)S(1)}, bf16[11,4096]{1,0:T(8,128)(2,1)S(1)}) custom-call(bf16[512,64]{1,0:T(8,128)(2,1)S(1)} %copy.13.tok_ref, bf16[512,64]{1,0:T(8,128)(2,1)S(1)} %copy.14.cot_ref, bf16[1,4096]{1,0:T(2,128)(2,1)S(1)} %reshape.11.gain_ref, ...), custom_call_target="tpu_custom_call" | custom-call | flops 1845493760 | bytes 8388608 | tf_op jit(solution)/shard_map/gather_and_grads/pallas_call | solution.py:367
  82.9 0.9 %copy.19 = bf16[1,88,4096]{2,1,0:T(8,128)(2,1)} copy(bf16[1,88,4096]{2,1,0:T(8,128)(2,1)S(1)} %bitcast.7) | data formatting | bytes 1441792
  83.7 0.9 copy.20
  84.6 0.7 copy.21
  85.3 0.7 copy.22
Async XLA Ops:
  0.6 2.7 %copy-start.4 = (f32[11,4096]{1,0:T(8,128)S(1)}, f32[11,4096]{1,0:T(8,128)}, u32[]{:S(2)}) copy-start(f32[11,4096]{1,0:T(8,128)} %mom_ref.1) | copy-start | bytes 540676
  2.4 1.0 %copy-start.5 = (bf16[11,4096]{1,0:T(8,128)(2,1)S(1)}, bf16[11,4096]{1,0:T(8,128)(2,1)}, u32[]{:S(2)}) copy-start(bf16[11,4096]{1,0:T(8,128)(2,1)} %anchor_ref.1) | copy-start | bytes 270340
  3.4 1.1 %copy-start = (bf16[1,88,4096]{2,1,0:T(8,128)(2,1)S(1)}, bf16[1,88,4096]{2,1,0:T(8,128)(2,1)}, u32[]{:S(2)}) copy-start(bf16[1,88,4096]{2,1,0:T(8,128)(2,1)} %param.11) | copy-start | bytes 2162692
  4.5 1.1 %copy-start.1 = (bf16[1,88,4096]{2,1,0:T(8,128)(2,1)S(1)}, bf16[1,88,4096]{2,1,0:T(8,128)(2,1)}, u32[]{:S(2)}) copy-start(bf16[1,88,4096]{2,1,0:T(8,128)(2,1)} %param.12) | copy-start | bytes 2162692
  5.6 1.1 %copy-start.2 = (bf16[1,88,4096]{2,1,0:T(8,128)(2,1)S(1)}, bf16[1,88,4096]{2,1,0:T(8,128)(2,1)}, u32[]{:S(2)}) copy-start(bf16[1,88,4096]{2,1,0:T(8,128)(2,1)} %param.13) | copy-start | bytes 2162692
  6.7 1.1 %copy-start.3 = (bf16[1,88,4096]{2,1,0:T(8,128)(2,1)S(1)}, bf16[1,88,4096]{2,1,0:T(8,128)(2,1)}, u32[]{:S(2)}) copy-start(bf16[1,88,4096]{2,1,0:T(8,128)(2,1)} %param.15) | copy-start | bytes 2162692

commit v2 on v1

v2 whole, which is shorter than its diff:
```python
import functools

import jax
import jax.numpy as jnp
from jax import lax
from jax.experimental import pallas as pl
from jax.experimental.pallas import tpu as pltpu
from jax.sharding import PartitionSpec as P

norm_epsilon = 1e-06
outer_beta = 0.9
outer_rate = 0.7

MESH = pl.DeviceIdType.MESH
F32 = jnp.float32
BF16 = jnp.bfloat16
D = 4096
HID = 88
NT = (((1,), (1,)), ((), ()))
NN = (((1,), (0,)), ((), ()))
TOK, COT = 0, 1
ORDER = (
    ('F', 0, 0), ('Z', 0), ('PG',), ('S', 1, 0, 0), ('F', 1, 0), ('S', 0, 0, 0), ('Z', 1), ('FF', 0, 0),
    ('FF', 1, 0), ('OP',), ('SF', 0, 0, 0), ('SF', 1, 0, 0), ('S', 0, 0, 1), ('S', 1, 0, 1), ('ZF', 0),
    ('F', 0, 1), ('F', 0, 3), ('S', 0, 1, 0), ('S', 0, 3, 0), ('PU',), ('SF', 0, 0, 1), ('SF', 1, 0, 1),
    ('FF', 0, 3), ('SF', 0, 1, 0), ('FF', 0, 1), ('ZF', 1), ('SF', 0, 3, 0), ('S', 1, 3, 0), ('F', 1, 1),
    ('F', 1, 3), ('S', 0, 3, 1), ('F', 0, 2), ('S', 0, 2, 0), ('OL',), ('FF', 1, 1), ('FF', 1, 3),
    ('S', 0, 1, 1), ('F', 1, 2), ('FF', 0, 2), ('PD',), ('S', 1, 3, 1), ('SF', 0, 3, 1), ('S', 0, 2, 1),
    ('SF', 0, 2, 0), ('SQ', 0, 0), ('FF', 1, 2), ('S', 1, 1, 0), ('S', 1, 1, 1), ('SF', 0, 1, 1),
    ('BW', 1, 0), ('SQ', 0, 3), ('SF', 0, 2, 1), ('S', 1, 2, 0), ('S', 1, 2, 1), ('SF', 1, 1, 0),
    ('SF', 1, 1, 1), ('OF',), ('SF', 1, 3, 1), ('SF', 1, 3, 0), ('SQ', 0, 1), ('SQ', 0, 2), ('FW', 0),
    ('SF', 1, 2, 0), ('FW', 1), ('SF', 1, 2, 1), ('FW', 2), ('BW', 1, 1), ('FW', 3), ('BW', 1, 3),
    ('BW', 1, 2),
)
GROUPS = {
    (0, 0): ((0, 1), (1, 4)),
    (1, 0): ((0, 1), (1, 4)),
    (0, 3): ((0, 1), (1, 4)),
    (0, 1): ((0, 1), (1, 4)),
    (1, 3): ((0, 1), (1, 4)),
    (0, 2): ((0, 1), (1, 4)),
    (1, 1): ((0, 1), (1, 4)),
    (1, 2): ((0, 1), (1, 4)),
}
COPIES = 4 + 4 * max(len(groups) for groups in GROUPS.values())


def kernel(
    tok_hbm, cot_hbm, gain_ref, gate_hbm, up_hbm, down_hbm, delta_hbm,
    d_out, normed_out, total_out,
    g, normed, gate_w, up_w, down_w, delta_v, gate_up, down_z, acc_pre, acc_back, squares, gain_v,
    share, pair_in, pair_out, line_in,
    load_sem, own_sem, out_sem, send, recv, zsend, zrecv, osend, orecv,
):
    f = lax.axis_index("fsdp")
    r = lax.axis_index("rep")
    y, x, zh = f // 16, (f // 4) % 4, f % 4
    zl, core = r // 2, r % 2

    def at(yy, xx, zz):
        return {"fsdp": ((yy + 4) % 4) * 16 + ((xx + 4) % 4) * 4 + (zz + 4) % 4}

    xn = (at(y, x + 1, zh), at(y, x - 1, zh))
    yn = (at(y + 1, x, zh), at(y - 1, x, zh))
    zn = (at(y, x, zh + 1), at(y, x, zh - 1))
    partner = {"rep": zl * 2 + 1 - core}
    line = [{"rep": ((zl + k) % 4) * 2 + core} for k in (1, 2, 3)]

    own = [
        pltpu.make_async_copy(ref.at[:, pl.ds(256 * h, 256)], g.at[t, h, 0, 0, 0], own_sem.at[t, h])
        for t, ref in ((TOK, tok_hbm), (COT, cot_hbm))
        for h in range(2)
    ]
    loads = [
        pltpu.make_async_copy(src, dst, load_sem.at[i])
        for i, (src, dst) in enumerate(
            ((delta_hbm, delta_v), (gate_hbm, gate_w), (up_hbm, up_w), (down_hbm, down_w))
        )
    ]
    for load in own:
        load.start()
    barrier = pltpu.get_barrier_semaphore()
    peers = [*zn, *line, partner, *xn, *yn]
    for peer in peers:
        pl.semaphore_signal(barrier, inc=1, device_id=peer, device_id_type=MESH)
    for load in own:
        load.wait()
    pl.semaphore_wait(barrier, len(peers))

    started, arrived = {}, set()

    def start(key, src, dst, ssem, rsem, device):
        copy = pltpu.make_async_remote_copy(
            src_ref=src, dst_ref=dst, send_sem=ssem, recv_sem=rsem,
            device_id=device, device_id_type=MESH,
        )
        copy.start()
        started[key] = copy

    def need(key):
        if key not in arrived:
            arrived.add(key)
            started[key].wait_recv()

    def xy(task, h, k, src, dst, device):
        t, rz = task
        start((task, h, k), src, dst, send.at[t, h, rz, k], recv.at[t, h, rz, k], device)

    def near(h):
        return (xn, yn) if h == 0 else (yn, xn)

    lo, hi = pl.ds(0, 32), pl.ds(32, 32)

    def first_send(task):
        for h in range(2):
            b = g.at[task[0], h, task[1]]
            xy(task, h, 0, b.at[0, 0], b.at[0, 3], near(h)[0][0])
            xy(task, h, 1, b.at[0, 0], b.at[0, 1], near(h)[0][1])

    def first_forward(task):
        for h in range(2):
            b = g.at[task[0], h, task[1]]
            need((task, h, 0))
            xy(task, h, 2, b.at[0, 3, lo], b.at[0, 2, lo], near(h)[0][0])
            need((task, h, 1))
            xy(task, h, 3, b.at[0, 1, hi], b.at[0, 2, hi], near(h)[0][1])

    brings = {0: (), 1: (1,), 2: (2, 3), 3: (0,)}

    def second_send(task, i):
        first, last = GROUPS[task][i]
        for h in range(2):
            b = g.at[task[0], h, task[1]]
            for offset in range(first, last):
                for k in brings[offset]:
                    need((task, h, k))
            cols = pl.ds(first, last - first)
            xy(task, h, 4 + 4 * i, b.at[0, cols], b.at[3, cols], near(h)[1][0])
            xy(task, h, 5 + 4 * i, b.at[0, cols], b.at[1, cols], near(h)[1][1])

    def second_forward(task, i):
        first, last = GROUPS[task][i]
        for h in range(2):
            b = g.at[task[0], h, task[1]]
            cols = pl.ds(first, last - first)
            need((task, h, 4 + 4 * i))
            xy(task, h, 6 + 4 * i, b.at[3, cols, lo], b.at[2, cols, lo], near(h)[1][0])
            need((task, h, 5 + 4 * i))
            xy(task, h, 7 + 4 * i, b.at[1, cols, hi], b.at[2, cols, hi], near(h)[1][1])

    def z_send(t):
        for h in range(2):
            start(("z", t, h, 0), g.at[t, h, 0, 0, 0], g.at[t, h, 3, 0, 0],
                  zsend.at[t, h, 0], zrecv.at[t, h, 0], zn[0])
        for h in (1, 0):
            start(("z", t, h, 1), g.at[t, h, 0, 0, 0], g.at[t, h, 1, 0, 0],
                  zsend.at[t, h, 1], zrecv.at[t, h, 1], zn[1])

    def z_forward(t):
        need(("z", t, 0, 0))
        start(("z", t, 0, 2), g.at[t, 0, 3, 0, 0], g.at[t, 0, 2, 0, 0],
              zsend.at[t, 0, 2], zrecv.at[t, 0, 2], zn[0])
        need(("z", t, 1, 1))
        start(("z", t, 1, 2), g.at[t, 1, 1, 0, 0], g.at[t, 1, 2, 0, 0],
              zsend.at[t, 1, 2], zrecv.at[t, 1, 2], zn[1])

    def z_need(task):
        t, rz = task
        if rz:
            for h in range(2):
                need(("z", t, h, {3: 0, 1: 1, 2: 2}[rz]))

    sent = set()

    def arrive(task):
        for h in range(2):
            for i in range(len(GROUPS[task])):
                need((task, h, 6 + 4 * i))
                need((task, h, 7 + 4 * i))
        for key, copy in started.items():
            if key[0] == task and key not in sent:
                sent.add(key)
                copy.wait_send()

    def outer_pack():
        loads[0].wait()

        @pl.loop(0, 8)
        def _(c):
            cols = pl.ds(pl.multiple_of(c * 512, 512), 512)
            rows = delta_v[:, cols].astype(F32)
            for b in range(8):
                if b < 7:
                    block = rows[b * 11 : b * 11 + 16]
                else:
                    block = jnp.concatenate([rows[77:88], jnp.zeros((5, 512), F32)], axis=0)
                share[b % 2, b // 2, :, cols] = block.astype(BF16)

    def outer_pair():
        start("pair", share.at[1 - core], pair_in, osend.at[0], orecv.at[0], partner)

    def outer_line():
        need("pair")

        @pl.loop(0, 4)
        def _(b):
            pair_out[b] = (share[core, b].astype(F32) + pair_in[b].astype(F32)).astype(BF16)

        for k in range(3):
            start(("line", k), pair_out.at[(zl + k + 1) % 4], line_in.at[k],
                  osend.at[1 + k], orecv.at[1 + k], line[k])

    def outer_finish():
        for k in range(3):
            need(("line", k))
        total = share[core, zl].astype(F32) + pair_in[zl].astype(F32)
        for k in range(3):
            total = total + line_in[k].astype(F32)
        total_out[...] = total

    def prep_gate_up():
        loads[1].wait()
        loads[2].wait()

        @pl.loop(0, 8)
        def _(c):
            cols = pl.ds(pl.multiple_of(c * 512, 512), 512)
            gate_up[:, cols] = jnp.concatenate(
                [gate_w[:, cols].astype(F32), up_w[:, cols].astype(F32)], axis=0
            ).astype(BF16)

    def prep_gain():
        @pl.loop(0, 16)
        def _(c):
            cols = pl.ds(pl.multiple_of(c * 256, 256), 256)
            row = gain_ref[cols].astype(F32)
            gain_v[cols, :] = jnp.broadcast_to(row[None, :], (128, 256)).T

        acc_back[...] = jnp.zeros_like(acc_back)
        acc_pre[...] = jnp.zeros_like(acc_pre)
        squares[...] = jnp.zeros_like(squares)

    def prep_down():
        loads[3].wait()
        low = lax.broadcasted_iota(jnp.int32, (HID, 128), 1) < 64

        @pl.loop(0, 4)
        def _(yy):
            for pair in range(2):
                for xs in range(2):
                    a, b = (
                        down_w[
                            :, pl.ds(pl.multiple_of((yy * 4 + xx) * 256 + pair * 128, 128), 128)
                        ].astype(F32)
                        for xx in (2 * xs, 2 * xs + 1)
                    )
                    lanes = pl.ds(xs * 128, 128)
                    down_z[2 * pair, yy, :, lanes] = jnp.where(low, a, pltpu.roll(b, 64, 1)).astype(BF16)
                    down_z[2 * pair + 1, yy, :, lanes] = jnp.where(low, pltpu.roll(a, 64, 1), b).astype(BF16)

    def block_of(t, rz, ry, rx):
        return jnp.concatenate([g[t, 0, rz, ry, rx], g[t, 1, rz, rx, ry]], axis=1)

    def add_squares(task):
        arrive(task)

        @pl.loop(0, 16)
        def _(b):
            v = block_of(TOK, task[1], b // 4, b % 4).astype(F32)
            v = v * v
            part = v[:8]
            for i in range(1, 8):
                part = part + v[8 * i : 8 * i + 8]
            squares[...] += part

    def inverse_scale():
        total = jnp.sum(squares[...], axis=0, keepdims=True)
        squares[...] = jnp.broadcast_to(1.0 / jnp.sqrt(total / D + norm_epsilon), squares.shape)

    def normed_copy(b):
        rows = pl.ds(pl.multiple_of(b * 256, 256), 256)
        return pltpu.make_async_copy(normed.at[rows], normed_out.at[rows], out_sem.at[b])

    def forward(first, last):
        @pl.loop(first, last)
        def _(b):
            ry, rx = (b // 4 - y + 4) % 4, (b % 4 - x + 4) % 4
            cols = pl.ds(pl.multiple_of(b * 256, 256), 256)
            scale = squares[0:1, :]
            gain = gain_v[cols, :]
            gain = jnp.concatenate([gain] * 4, axis=1)
            raw = jnp.concatenate(
                [block_of(TOK, (zs - zh + 4) % 4, ry, rx) for zs in range(4)], axis=0
            )
            block = (raw.astype(F32) * scale * gain).astype(BF16)
            normed[cols, :] = block
            normed_copy(b).start()
            acc_pre[...] += lax.dot_general(
                gate_up[:, cols], block, NN, preferred_element_type=F32
            )

    def backward(task):
        arrive(task)
        rz = task[1]
        zs = (zh + rz) % 4

        @pl.loop(0, 4)
        def _(yy):
            ry = (yy - y + 4) % 4
            rows = jnp.concatenate(
                [block_of(COT, rz, ry, (xx - x + 4) % 4) for xx in range(4)], axis=0
            )
            acc_back[...] += lax.dot_general(
                down_z[zs, yy], rows, NN, preferred_element_type=F32
            )

    def finish():
        for q in range(4):
            lanes = pl.ds(q * 128, 128)
            gate_pre = acc_pre[:HID, lanes]
            up_pre = acc_pre[HID:, lanes]
            back = acc_back[:, lanes]
            sig = jax.nn.sigmoid(gate_pre)
            d_gate = back * up_pre * sig * (1.0 + gate_pre * (1.0 - sig))
            d_up = back * gate_pre * sig
            d_out[:, lanes] = jnp.concatenate([d_gate, d_up], axis=0).astype(BF16)

    def run(op):
        name, args = op[0], op[1:]
        task = args[:2]
        if name == "Z":
            z_send(args[0])
        elif name == "ZF":
            z_forward(args[0])
        elif name == "F":
            z_need(task)
            first_send(task)
        elif name == "FF":
            first_forward(task)
        elif name == "S":
            z_need(task)
            second_send(task, args[2])
        elif name == "SF":
            second_forward(task, args[2])
        elif name == "OP":
            outer_pack()
            outer_pair()
        elif name == "OL":
            outer_line()
        elif name == "OF":
            outer_finish()
        elif name == "PG":
            prep_gain()
        elif name == "PD":
            prep_down()
        elif name == "PU":
            prep_gate_up()
        elif name == "SQ":
            add_squares(task)
        elif name == "FW":
            if args[0] == 0:
                inverse_scale()
            forward(4 * args[0], 4 * args[0] + 4)
        elif name == "BW":
            backward(task)

    for i, op in enumerate(ORDER):
        if i == 3:
            for load in loads:
                load.start()
        run(op)
    finish()
    for b in range(16):
        normed_copy(b).wait()
    for key, copy in started.items():
        if key not in sent:
            copy.wait_send()


CHUNKS = 8


def finish_kernel(
    d_ref, normed_hbm, total_ref, mom_ref, anchor_ref,
    grad_gate, grad_up, new_mom, new_anchor,
    normed, gate_v, up_v, in_sem, out_sem,
):
    wide = D // CHUNKS
    reads = [
        pltpu.make_async_copy(
            normed_hbm.at[pl.ds(c * wide, wide)], normed.at[pl.ds(c * wide, wide)], in_sem.at[c]
        )
        for c in range(CHUNKS)
    ]
    for read in reads:
        read.start()
    mean_delta = total_ref[:11] / 8.0
    momentum = outer_beta * mom_ref[...] + mean_delta
    new_mom[...] = momentum
    new_anchor[...] = (
        anchor_ref[...].astype(F32) - outer_rate * (mean_delta + outer_beta * momentum)
    ).astype(BF16)
    writes = []
    for c in range(CHUNKS):
        cols = pl.ds(c * wide, wide)
        reads[c].wait()
        out = lax.dot_general(d_ref[...], normed[cols, :], NT, preferred_element_type=F32)
        gate_v[:, cols] = out[:HID].astype(BF16)
        up_v[:, cols] = out[HID:].astype(BF16)
        for i, (src, dst) in enumerate(((gate_v, grad_gate), (up_v, grad_up))):
            writes.append(
                pltpu.make_async_copy(src.at[:, cols], dst.at[:, cols], out_sem.at[c, i])
            )
            writes[-1].start()
    for write in writes:
        write.wait()


def body(
    tokens, norm_gain, gate_weight, up_weight, down_weight, cotangent, outer_delta, momentum, anchor
):
    vmem = pl.BlockSpec(memory_space=pltpu.VMEM)
    hbm = pl.BlockSpec(memory_space=pltpu.HBM)
    dma = pltpu.SemaphoreType.DMA
    d_t, normed, total = pl.pallas_call(
        kernel,
        out_shape=(
            jax.ShapeDtypeStruct((2 * HID, 512), BF16),
            jax.ShapeDtypeStruct((D, 512), BF16),
            jax.ShapeDtypeStruct((16, D), F32),
        ),
        in_specs=[hbm, hbm, vmem, hbm, hbm, hbm, hbm],
        out_specs=(vmem, hbm, vmem),
        scratch_shapes=[
            pltpu.VMEM((2, 2, 4, 4, 4, 64, 256), BF16),
            pltpu.VMEM((D, 512), BF16),
            pltpu.VMEM((HID, D), BF16),
            pltpu.VMEM((HID, D), BF16),
            pltpu.VMEM((HID, D), BF16),
            pltpu.VMEM((HID, D), BF16),
            pltpu.VMEM((2 * HID, D), BF16),
            pltpu.VMEM((4, 4, HID, 256), BF16),
            pltpu.VMEM((2 * HID, 512), F32),
            pltpu.VMEM((HID, 512), F32),
            pltpu.VMEM((8, 512), F32),
            pltpu.VMEM((D, 128), F32),
            pltpu.VMEM((2, 4, 16, D), BF16),
            pltpu.VMEM((4, 16, D), BF16),
            pltpu.VMEM((4, 16, D), BF16),
            pltpu.VMEM((3, 16, D), BF16),
            dma((4,)),
            dma((2, 2)),
            dma((16,)),
            dma((2, 2, 4, COPIES)),
            dma((2, 2, 4, COPIES)),
            dma((2, 2, 3)),
            dma((2, 2, 3)),
            dma((4,)),
            dma((4,)),
        ],
        compiler_params=pltpu.CompilerParams(
            collective_id=0, has_side_effects=True, vmem_limit_bytes=62 * 2**20
        ),
        cost_estimate=pl.CostEstimate(
            flops=6 * 512 * D * HID, bytes_accessed=8 * 2**20, transcendentals=512 * HID
        ),
        name="gather_and_forward",
    )(
        tokens.T, cotangent.T, norm_gain, gate_weight[0], up_weight[0], down_weight[0],
        outer_delta[0],
    )
    outs = pl.pallas_call(
        finish_kernel,
        out_shape=(
            jax.ShapeDtypeStruct((HID, D), BF16),
            jax.ShapeDtypeStruct((HID, D), BF16),
            jax.ShapeDtypeStruct((11, D), F32),
            jax.ShapeDtypeStruct((11, D), BF16),
        ),
        in_specs=[vmem, hbm, vmem, vmem, vmem],
        out_specs=(hbm, hbm, vmem, vmem),
        scratch_shapes=[
            pltpu.VMEM((D, 512), BF16),
            pltpu.VMEM((HID, D), BF16),
            pltpu.VMEM((HID, D), BF16),
            dma((CHUNKS,)),
            dma((CHUNKS, 2)),
        ],
        compiler_params=pltpu.CompilerParams(vmem_limit_bytes=62 * 2**20),
        cost_estimate=pl.CostEstimate(
            flops=4 * 512 * D * HID, bytes_accessed=6 * 2**20, transcendentals=0
        ),
        name="gradients_and_outer_update",
    )(d_t, normed, total, momentum, anchor)
    return outs[0][None], outs[1][None], outs[2], outs[3]


def solution(mesh):
    return jax.shard_map(
        body,
        mesh=mesh,
        in_specs=(
            P("rep", "fsdp"),
            P(),
            P("rep", "fsdp", None),
            P("rep", "fsdp", None),
            P("rep", "fsdp", None),
            P("rep", "fsdp"),
            P("rep", "fsdp", None),
            P(("fsdp", "rep"), None),
            P(("fsdp", "rep"), None),
        ),
        out_specs=(
            P("rep", "fsdp", None),
            P("rep", "fsdp", None),
            P(("fsdp", "rep"), None),
            P(("fsdp", "rep"), None),
        ),
        check_vma=False,
    )
```

time: 86.3 us -> 74.9 us (0.87)
  the two profiles are of different devices: /device:TPU:32 before, /device:TPU:6 now
where the time goes in v2:
time: 74.9 us; the launch traced here: 74.5 us
  Pallas kernels  73.8 us (99%)
    pallas_call x1, Pallas kernels, body(): pl.pallas_call(kernel, out_shape=(jax.ShapeDtypeStruct((2 * HID, 512), BF...  67.5 us
    pallas_call x1, Pallas kernels, body(): pl.pallas_call(finish_kernel, out_shape=(jax.ShapeDtypeStruct((HID, D), B...  6.39 us

profile of v2, /device:TPU:6, one launch (start us, length us, event | category | flops | bytes accessed | tf_op | source)
XLA Modules:
  0.0 74.5 jit_solution(5753344990244607447)
XLA Ops:
  0.6 67.5 %gather_and_forward.1 = (bf16[176,512]{1,0:T(8,128)(2,1)}, bf16[4096,512]{1,0:T(8,128)(2,1)}, f32[16,4096]{1,0:T(8,128)}) custom-call(bf16[64,512]{1,0:T(8,128)(2,1)} %bitcast.14, bf16[64,512]{1,0:T(8,128)(2,1)} %bitcast.15, bf16[4096]{0:T(1024)(128)(2,1)} %gain_ref.1, bf16[88,4096]{1,0:T(8,128)(2,1)} %bitcast.8, bf16[88,4096]{1,0:T(8,128)(2,1)} %bitcast.9, ...), custom_call_target="tpu_custom_call" | custom-call | flops 1107296256 | bytes 8388608 | tf_op jit(solution)/shard_map/gather_and_forward/pallas_call | solution.py:425
  68.1 6.4 %gradients_and_outer_update.1 = (bf16[88,4096]{1,0:T(8,128)(2,1)}, bf16[88,4096]{1,0:T(8,128)(2,1)}, f32[11,4096]{1,0:T(8,128)}, bf16[11,4096]{1,0:T(8,128)(2,1)}) custom-call(bf16[176,512]{1,0:T(8,128)(2,1)} %get-tuple-element.11.d_ref, bf16[4096,512]{1,0:T(8,128)(2,1)} %get-tuple-element.12.normed_hbm, f32[16,4096]{1,0:T(8,128)} %get-tuple-element.13.total_ref, ...), custom_call_target="tpu_custom_call" | custom-call | flops 738197504 | bytes 6291456 | tf_op jit(solution)/shard_map/gradients_and_outer_update/pallas_call | solution.py:472

commit v3 on v2

--- a/solution.py
+++ b/solution.py
@@ -20,17 +20,16 @@
 NN = (((1,), (0,)), ((), ()))
 TOK, COT = 0, 1
 ORDER = (
-    ('F', 0, 0), ('Z', 0), ('PG',), ('S', 1, 0, 0), ('F', 1, 0), ('S', 0, 0, 0), ('Z', 1), ('FF', 0, 0),
-    ('FF', 1, 0), ('OP',), ('SF', 0, 0, 0), ('SF', 1, 0, 0), ('S', 0, 0, 1), ('S', 1, 0, 1), ('ZF', 0),
-    ('F', 0, 1), ('F', 0, 3), ('S', 0, 1, 0), ('S', 0, 3, 0), ('PU',), ('SF', 0, 0, 1), ('SF', 1, 0, 1),
-    ('FF', 0, 3), ('SF', 0, 1, 0), ('FF', 0, 1), ('ZF', 1), ('SF', 0, 3, 0), ('S', 1, 3, 0), ('F', 1, 1),
-    ('F', 1, 3), ('S', 0, 3, 1), ('F', 0, 2), ('S', 0, 2, 0), ('OL',), ('FF', 1, 1), ('FF', 1, 3),
-    ('S', 0, 1, 1), ('F', 1, 2), ('FF', 0, 2), ('PD',), ('S', 1, 3, 1), ('SF', 0, 3, 1), ('S', 0, 2, 1),
-    ('SF', 0, 2, 0), ('SQ', 0, 0), ('FF', 1, 2), ('S', 1, 1, 0), ('S', 1, 1, 1), ('SF', 0, 1, 1),
-    ('BW', 1, 0), ('SQ', 0, 3), ('SF', 0, 2, 1), ('S', 1, 2, 0), ('S', 1, 2, 1), ('SF', 1, 1, 0),
-    ('SF', 1, 1, 1), ('OF',), ('SF', 1, 3, 1), ('SF', 1, 3, 0), ('SQ', 0, 1), ('SQ', 0, 2), ('FW', 0),
-    ('SF', 1, 2, 0), ('FW', 1), ('SF', 1, 2, 1), ('FW', 2), ('BW', 1, 1), ('FW', 3), ('BW', 1, 3),
-    ('BW', 1, 2),
+    ('F', 1, 0), ('Z', 0), ('S', 1, 0, 0), ('F', 0, 0), ('S', 0, 0, 0), ('FF', 1, 0), ('FF', 0, 0), ('PG',),
+    ('Z', 1), ('SF', 0, 0, 0), ('SF', 1, 0, 0), ('S', 1, 0, 1), ('S', 0, 0, 1), ('PD',), ('S', 0, 1, 0),
+    ('ZF', 0), ('F', 0, 1), ('S', 0, 3, 0), ('SF', 1, 0, 1), ('F', 0, 3), ('SF', 0, 0, 1), ('SF', 0, 1, 0),
+    ('ZF', 1), ('SF', 0, 3, 0), ('FF', 0, 1), ('F', 1, 3), ('OP',), ('F', 1, 1), ('S', 1, 3, 0),
+    ('S', 1, 1, 0), ('FF', 0, 3), ('S', 0, 2, 0), ('F', 0, 2), ('S', 0, 1, 1), ('OL',), ('S', 0, 3, 1),
+    ('FF', 0, 2), ('FF', 1, 1), ('F', 1, 2), ('SF', 0, 2, 0), ('FF', 1, 3), ('S', 1, 2, 0), ('SF', 0, 1, 1),
+    ('BW', 1, 0), ('S', 0, 2, 1), ('SF', 0, 3, 1), ('FF', 1, 2), ('SQ', 0, 0), ('PU',), ('S', 1, 1, 1),
+    ('SF', 0, 2, 1), ('S', 1, 3, 1), ('S', 1, 2, 1), ('SQ', 0, 1), ('SQ', 0, 3), ('SF', 1, 1, 0),
+    ('SF', 1, 2, 0), ('SQ', 0, 2), ('SF', 1, 1, 1), ('SF', 1, 3, 0), ('FW', 0), ('FW', 1), ('SF', 1, 3, 1),
+    ('SF', 1, 2, 1), ('FW', 2), ('FW', 3), ('OF',), ('BW', 1, 1), ('BW', 1, 3), ('BW', 1, 2),
 )
 GROUPS = {
     (0, 0): ((0, 1), (1, 4)),
@@ -46,11 +45,11 @@
 
 
 def kernel(
-    tok_hbm, cot_hbm, gain_ref, gate_hbm, up_hbm, down_hbm, delta_hbm,
-    d_out, normed_out, total_out,
-    g, normed, gate_w, up_w, down_w, delta_v, gate_up, down_z, acc_pre, acc_back, squares, gain_v,
+    tok_hbm, cot_hbm, gain_hbm, gate_hbm, up_hbm, down_hbm, delta_hbm,
+    d_out, normed, total_out,
+    g, gate_w, up_w, down_w, delta_v, gate_up, down_z, acc_pre, acc_back, squares, gain_v, gain_ref,
     share, pair_in, pair_out, line_in,
-    load_sem, own_sem, out_sem, send, recv, zsend, zrecv, osend, orecv,
+    load_sem, own_sem, send, recv, zsend, zrecv, osend, orecv,
 ):
     f = lax.axis_index("fsdp")
     r = lax.axis_index("rep")
@@ -66,15 +65,18 @@
     partner = {"rep": zl * 2 + 1 - core}
     line = [{"rep": ((zl + k) % 4) * 2 + core} for k in (1, 2, 3)]
 
+    def mine(t, h):
+        return (tok_hbm, cot_hbm)[t].at[:, pl.ds(256 * h, 256)]
+
     own = [
-        pltpu.make_async_copy(ref.at[:, pl.ds(256 * h, 256)], g.at[t, h, 0, 0, 0], own_sem.at[t, h])
-        for t, ref in ((TOK, tok_hbm), (COT, cot_hbm))
+        pltpu.make_async_copy(mine(t, h), g.at[t, h, 0, 0, 0], own_sem.at[t, h])
+        for t in (TOK, COT)
         for h in range(2)
     ]
     loads = [
         pltpu.make_async_copy(src, dst, load_sem.at[i])
         for i, (src, dst) in enumerate(
-            ((delta_hbm, delta_v), (gate_hbm, gate_w), (up_hbm, up_w), (down_hbm, down_w))
+            ((delta_hbm, delta_v), (gate_hbm, gate_w), (up_hbm, up_w), (down_hbm, down_w), (gain_hbm, gain_ref))
         )
     ]
     for load in own:
@@ -114,8 +116,9 @@
     def first_send(task):
         for h in range(2):
             b = g.at[task[0], h, task[1]]
-            xy(task, h, 0, b.at[0, 0], b.at[0, 3], near(h)[0][0])
-            xy(task, h, 1, b.at[0, 0], b.at[0, 1], near(h)[0][1])
+            src = b.at[0, 0]
+            xy(task, h, 0, src, b.at[0, 3], near(h)[0][0])
+            xy(task, h, 1, src, b.at[0, 1], near(h)[0][1])
 
     def first_forward(task):
         for h in range(2):
@@ -135,8 +138,9 @@
                 for k in brings[offset]:
                     need((task, h, k))
             cols = pl.ds(first, last - first)
-            xy(task, h, 4 + 4 * i, b.at[0, cols], b.at[3, cols], near(h)[1][0])
-            xy(task, h, 5 + 4 * i, b.at[0, cols], b.at[1, cols], near(h)[1][1])
+            src = b.at[0, cols]
+            xy(task, h, 4 + 4 * i, src, b.at[3, cols], near(h)[1][0])
+            xy(task, h, 5 + 4 * i, src, b.at[1, cols], near(h)[1][1])
 
     def second_forward(task, i):
         first, last = GROUPS[task][i]
@@ -230,11 +234,11 @@
             ).astype(BF16)
 
     def prep_gain():
-        @pl.loop(0, 16)
-        def _(c):
-            cols = pl.ds(pl.multiple_of(c * 256, 256), 256)
-            row = gain_ref[cols].astype(F32)
-            gain_v[cols, :] = jnp.broadcast_to(row[None, :], (128, 256)).T
+        loads[4].wait()
+
+        rows = gain_ref[...].astype(F32)
+        for c in range(32):
+            gain_v[c * 128 : c * 128 + 128, :] = jnp.broadcast_to(rows[c : c + 1], (128, 128)).T
 
         acc_back[...] = jnp.zeros_like(acc_back)
         acc_pre[...] = jnp.zeros_like(acc_pre)
@@ -277,10 +281,6 @@
         total = jnp.sum(squares[...], axis=0, keepdims=True)
         squares[...] = jnp.broadcast_to(1.0 / jnp.sqrt(total / D + norm_epsilon), squares.shape)
 
-    def normed_copy(b):
-        rows = pl.ds(pl.multiple_of(b * 256, 256), 256)
-        return pltpu.make_async_copy(normed.at[rows], normed_out.at[rows], out_sem.at[b])
-
     def forward(first, last):
         @pl.loop(first, last)
         def _(b):
@@ -294,7 +294,6 @@
             )
             block = (raw.astype(F32) * scale * gain).astype(BF16)
             normed[cols, :] = block
-            normed_copy(b).start()
             acc_pre[...] += lax.dot_general(
                 gate_up[:, cols], block, NN, preferred_element_type=F32
             )
@@ -370,8 +369,6 @@
                 load.start()
         run(op)
     finish()
-    for b in range(16):
-        normed_copy(b).wait()
     for key, copy in started.items():
         if key not in sent:
             copy.wait_send()
@@ -381,30 +378,15 @@
 
 
 def finish_kernel(
-    d_ref, normed_hbm, total_ref, mom_ref, anchor_ref,
+    d_ref, normed_ref, total_ref, mom_ref, anchor_ref,
     grad_gate, grad_up, new_mom, new_anchor,
-    normed, gate_v, up_v, in_sem, out_sem,
+    gate_v, up_v, out_sem,
 ):
     wide = D // CHUNKS
-    reads = [
-        pltpu.make_async_copy(
-            normed_hbm.at[pl.ds(c * wide, wide)], normed.at[pl.ds(c * wide, wide)], in_sem.at[c]
-        )
-        for c in range(CHUNKS)
-    ]
-    for read in reads:
-        read.start()
-    mean_delta = total_ref[:11] / 8.0
-    momentum = outer_beta * mom_ref[...] + mean_delta
-    new_mom[...] = momentum
-    new_anchor[...] = (
-        anchor_ref[...].astype(F32) - outer_rate * (mean_delta + outer_beta * momentum)
-    ).astype(BF16)
     writes = []
     for c in range(CHUNKS):
         cols = pl.ds(c * wide, wide)
-        reads[c].wait()
-        out = lax.dot_general(d_ref[...], normed[cols, :], NT, preferred_element_type=F32)
+        out = lax.dot_general(d_ref[...], normed_ref[cols, :], NT, preferred_element_type=F32)
         gate_v[:, cols] = out[:HID].astype(BF16)
         up_v[:, cols] = out[HID:].astype(BF16)
         for i, (src, dst) in enumerate(((gate_v, grad_gate), (up_v, grad_up))):
@@ -412,6 +394,12 @@
                 pltpu.make_async_copy(src.at[:, cols], dst.at[:, cols], out_sem.at[c, i])
             )
             writes[-1].start()
+    mean_delta = total_ref[:11] / 8.0
+    momentum = outer_beta * mom_ref[...] + mean_delta
+    new_mom[...] = momentum
+    new_anchor[...] = (
+        anchor_ref[...].astype(F32) - outer_rate * (mean_delta + outer_beta * momentum)
+    ).astype(BF16)
     for write in writes:
         write.wait()
 
@@ -425,15 +413,14 @@
     d_t, normed, total = pl.pallas_call(
         kernel,
         out_shape=(
-            jax.ShapeDtypeStruct((2 * HID, 512), BF16),
-            jax.ShapeDtypeStruct((D, 512), BF16),
-            jax.ShapeDtypeStruct((16, D), F32),
-        ),
-        in_specs=[hbm, hbm, vmem, hbm, hbm, hbm, hbm],
-        out_specs=(vmem, hbm, vmem),
+            pltpu.VMEM((2 * HID, 512), BF16),
+            pltpu.VMEM((D, 512), BF16),
+            pltpu.VMEM((16, D), F32),
+        ),
+        in_specs=[hbm] * 7,
+        out_specs=(vmem, vmem, vmem),
         scratch_shapes=[
             pltpu.VMEM((2, 2, 4, 4, 4, 64, 256), BF16),
-            pltpu.VMEM((D, 512), BF16),
             pltpu.VMEM((HID, D), BF16),
             pltpu.VMEM((HID, D), BF16),
             pltpu.VMEM((HID, D), BF16),
@@ -444,13 +431,13 @@
             pltpu.VMEM((HID, 512), F32),
             pltpu.VMEM((8, 512), F32),
             pltpu.VMEM((D, 128), F32),
+            pltpu.VMEM((32, 128), BF16),
             pltpu.VMEM((2, 4, 16, D), BF16),
             pltpu.VMEM((4, 16, D), BF16),
             pltpu.VMEM((4, 16, D), BF16),
             pltpu.VMEM((3, 16, D), BF16),
-            dma((4,)),
+            dma((5,)),
             dma((2, 2)),
-            dma((16,)),
             dma((2, 2, 4, COPIES)),
             dma((2, 2, 4, COPIES)),
             dma((2, 2, 3)),
@@ -459,15 +446,23 @@
             dma((4,)),
         ],
         compiler_params=pltpu.CompilerParams(
-            collective_id=0, has_side_effects=True, vmem_limit_bytes=62 * 2**20
+            collective_id=0, has_side_effects=True, vmem_limit_bytes=48 * 2**20
         ),
         cost_estimate=pl.CostEstimate(
             flops=6 * 512 * D * HID, bytes_accessed=8 * 2**20, transcendentals=512 * HID
         ),
         name="gather_and_forward",
     )(
-        tokens.T, cotangent.T, norm_gain, gate_weight[0], up_weight[0], down_weight[0],
-        outer_delta[0],
+        *(
+            pltpu.with_memory_space_constraint(a, pltpu.HBM)
+            for a in (
+                tokens.T, cotangent.T, norm_gain.reshape(32, 128), gate_weight[0], up_weight[0], down_weight[0],
+                outer_delta[0],
+            )
+        )
+    )
+    d_t, normed, total = (
+        pltpu.with_memory_space_constraint(a, pltpu.VMEM) for a in (d_t, normed, total)
     )
     outs = pl.pallas_call(
         finish_kernel,
@@ -477,16 +472,14 @@
             jax.ShapeDtypeStruct((11, D), F32),
             jax.ShapeDtypeStruct((11, D), BF16),
         ),
-        in_specs=[vmem, hbm, vmem, vmem, vmem],
+        in_specs=[vmem, vmem, vmem, vmem, vmem],
         out_specs=(hbm, hbm, vmem, vmem),
         scratch_shapes=[
-            pltpu.VMEM((D, 512), BF16),
             pltpu.VMEM((HID, D), BF16),
             pltpu.VMEM((HID, D), BF16),
-            dma((CHUNKS,)),
             dma((CHUNKS, 2)),
         ],
-        compiler_params=pltpu.CompilerParams(vmem_limit_bytes=62 * 2**20),
+        compiler_params=pltpu.CompilerParams(vmem_limit_bytes=16 * 2**20),
         cost_estimate=pl.CostEstimate(
             flops=4 * 512 * D * HID, bytes_accessed=6 * 2**20, transcendentals=0
         ),

time: 74.9 us -> 70 us (0.935)
  Pallas kernels: 73.8 us -> 69.2 us
    pallas_call x1, Pallas kernels: 6.39 us -> 3.06 us  [body(): pl.pallas_call(finish_kernel, out_shape=(jax.ShapeDtypeStruct((HID, D), B...]
    pallas_call x1, Pallas kernels: 67.5 us -> 66.1 us  [body(): pl.pallas_call(kernel, out_shape=(pltpu.VMEM((2 * HID, 512), BF16), pltpu...]
where the time goes in v3:
time: 70 us; the launch traced here: 69.8 us
  Pallas kernels  69.2 us (99%)
    pallas_call x1, Pallas kernels, body(): pl.pallas_call(kernel, out_shape=(pltpu.VMEM((2 * HID, 512), BF16), pltpu...  66.1 us
    pallas_call x1, Pallas kernels, body(): pl.pallas_call(finish_kernel, out_shape=(jax.ShapeDtypeStruct((HID, D), B...  3.06 us

profile of v3, /device:TPU:6, one launch (start us, length us, event | category | flops | bytes accessed | tf_op | source)
XLA Modules:
  0.0 69.8 jit_solution(14022321880308428708)
XLA Ops:
  0.6 0.0 copy-start.1
  0.6 0.0 copy-start
  0.7 66.1 %gather_and_forward.1 = (bf16[176,512]{1,0:T(8,128)(2,1)S(1)}, bf16[4096,512]{1,0:T(8,128)(2,1)S(1)}, f32[16,4096]{1,0:T(8,128)S(1)}) custom-call(bf16[64,512]{1,0:T(8,128)(2,1)} %bitcast.15, bf16[64,512]{1,0:T(8,128)(2,1)} %bitcast.16, bf16[32,128]{1,0:T(8,128)(2,1)} %bitcast.17, bf16[88,4096]{1,0:T(8,128)(2,1)} %bitcast.9, bf16[88,4096]{1,0:T(8,128)(2,1)} %bitcast.10, ...), custom_call_target="tpu_custom_call" | custom-call | flops 1107296256 | bytes 8388608 | tf_op jit(solution)/shard_map/gather_and_forward/pallas_call | solution.py:413
  66.8 0.0 copy-done.1
  66.8 0.0 copy-done
  66.8 3.1 %gradients_and_outer_update.1 = (bf16[88,4096]{1,0:T(8,128)(2,1)}, bf16[88,4096]{1,0:T(8,128)(2,1)}, f32[11,4096]{1,0:T(8,128)}, bf16[11,4096]{1,0:T(8,128)(2,1)}) custom-call(bf16[176,512]{1,0:T(8,128)(2,1)S(1)} %get-tuple-element.11.d_ref, bf16[4096,512]{1,0:T(8,128)(2,1)S(1)} %get-tuple-element.12.normed_ref, f32[16,4096]{1,0:T(8,128)S(1)} %get-tuple-element.13.total_ref, ...), custom_call_target="tpu_custom_call" | custom-call | flops 738197504 | bytes 6291456 | tf_op jit(solution)/shard_map/gradients_and_outer_update/pallas_call | solution.py:467
Async XLA Ops:
  0.6 66.1 %copy-start.1 = (bf16[11,4096]{1,0:T(8,128)(2,1)S(1)}, bf16[11,4096]{1,0:T(8,128)(2,1)}, u32[]{:S(2)}) copy-start(bf16[11,4096]{1,0:T(8,128)(2,1)} %anchor_ref.1) | copy-start | bytes 270340
  0.6 66.1 %copy-start = (f32[11,4096]{1,0:T(8,128)S(1)}, f32[11,4096]{1,0:T(8,128)}, u32[]{:S(2)}) copy-start(f32[11,4096]{1,0:T(8,128)} %mom_ref.1) | copy-start | bytes 540676

commit v4 on v3

--- a/solution.py
+++ b/solution.py
@@ -20,16 +20,17 @@
 NN = (((1,), (0,)), ((), ()))
 TOK, COT = 0, 1
 ORDER = (
-    ('F', 1, 0), ('Z', 0), ('S', 1, 0, 0), ('F', 0, 0), ('S', 0, 0, 0), ('FF', 1, 0), ('FF', 0, 0), ('PG',),
-    ('Z', 1), ('SF', 0, 0, 0), ('SF', 1, 0, 0), ('S', 1, 0, 1), ('S', 0, 0, 1), ('PD',), ('S', 0, 1, 0),
-    ('ZF', 0), ('F', 0, 1), ('S', 0, 3, 0), ('SF', 1, 0, 1), ('F', 0, 3), ('SF', 0, 0, 1), ('SF', 0, 1, 0),
-    ('ZF', 1), ('SF', 0, 3, 0), ('FF', 0, 1), ('F', 1, 3), ('OP',), ('F', 1, 1), ('S', 1, 3, 0),
-    ('S', 1, 1, 0), ('FF', 0, 3), ('S', 0, 2, 0), ('F', 0, 2), ('S', 0, 1, 1), ('OL',), ('S', 0, 3, 1),
-    ('FF', 0, 2), ('FF', 1, 1), ('F', 1, 2), ('SF', 0, 2, 0), ('FF', 1, 3), ('S', 1, 2, 0), ('SF', 0, 1, 1),
-    ('BW', 1, 0), ('S', 0, 2, 1), ('SF', 0, 3, 1), ('FF', 1, 2), ('SQ', 0, 0), ('PU',), ('S', 1, 1, 1),
-    ('SF', 0, 2, 1), ('S', 1, 3, 1), ('S', 1, 2, 1), ('SQ', 0, 1), ('SQ', 0, 3), ('SF', 1, 1, 0),
-    ('SF', 1, 2, 0), ('SQ', 0, 2), ('SF', 1, 1, 1), ('SF', 1, 3, 0), ('FW', 0), ('FW', 1), ('SF', 1, 3, 1),
-    ('SF', 1, 2, 1), ('FW', 2), ('FW', 3), ('OF',), ('BW', 1, 1), ('BW', 1, 3), ('BW', 1, 2),
+    ('F', 0, 0), ('Z', 0), ('S', 0, 0, 0), ('F', 1, 0), ('S', 1, 0, 0), ('FF', 0, 0), ('SF', 0, 0, 0),
+    ('FF', 1, 0), ('PG',), ('SF', 1, 0, 0), ('Z', 1), ('S', 0, 0, 1), ('S', 1, 0, 1), ('F', 0, 1),
+    ('F', 0, 3), ('ZF', 0), ('S', 0, 1, 0), ('SF', 0, 0, 1), ('OP',), ('SF', 1, 0, 1), ('FF', 0, 1),
+    ('S', 0, 3, 0), ('FF', 0, 3), ('ZF', 1), ('SF', 0, 1, 0), ('S', 1, 3, 0), ('F', 1, 3), ('F', 1, 1),
+    ('S', 0, 1, 1), ('PD',), ('OL',), ('SQ', 0, 0), ('F', 0, 2), ('S', 0, 2, 0), ('S', 0, 3, 1),
+    ('SF', 0, 1, 1), ('FF', 0, 2), ('F', 1, 2), ('S', 1, 1, 0), ('S', 1, 2, 0), ('SF', 0, 3, 0), ('FF', 1, 1),
+    ('SF', 0, 2, 0), ('FF', 1, 3), ('S', 0, 2, 1), ('FF', 1, 2), ('SF', 0, 3, 1), ('BW', 1, 0), ('PU',),
+    ('S', 1, 1, 1), ('SF', 0, 2, 1), ('S', 1, 3, 1), ('S', 1, 2, 1), ('SF', 1, 1, 0), ('SF', 1, 1, 1),
+    ('SQ', 0, 3), ('SQ', 0, 1), ('SQ', 0, 2), ('SF', 1, 2, 0), ('FW', 0), ('SF', 1, 3, 0), ('OF',),
+    ('SF', 1, 3, 1), ('FW', 1), ('SF', 1, 2, 1), ('FW', 2), ('FW', 3), ('BW', 1, 1), ('BW', 1, 3),
+    ('BW', 1, 2),
 )
 GROUPS = {
     (0, 0): ((0, 1), (1, 4)),
@@ -79,12 +80,13 @@
             ((delta_hbm, delta_v), (gate_hbm, gate_w), (up_hbm, up_w), (down_hbm, down_w), (gain_hbm, gain_ref))
         )
     ]
-    for load in own:
-        load.start()
     barrier = pltpu.get_barrier_semaphore()
-    peers = [*zn, *line, partner, *xn, *yn]
-    for peer in peers:
+    peers = [*xn, *yn, *zn, *line, partner]
+    for i, peer in enumerate(peers):
         pl.semaphore_signal(barrier, inc=1, device_id=peer, device_id_type=MESH)
+        if i == 5:
+            for load in own:
+                load.start()
     for load in own:
         load.wait()
     pl.semaphore_wait(barrier, len(peers))
@@ -293,7 +295,7 @@
                 [block_of(TOK, (zs - zh + 4) % 4, ry, rx) for zs in range(4)], axis=0
             )
             block = (raw.astype(F32) * scale * gain).astype(BF16)
-            normed[cols, :] = block
+            normed[:, cols] = block.T
             acc_pre[...] += lax.dot_general(
                 gate_up[:, cols], block, NN, preferred_element_type=F32
             )
@@ -386,7 +388,7 @@
     writes = []
     for c in range(CHUNKS):
         cols = pl.ds(c * wide, wide)
-        out = lax.dot_general(d_ref[...], normed_ref[cols, :], NT, preferred_element_type=F32)
+        out = lax.dot_general(d_ref[...], normed_ref[:, cols], NN, preferred_element_type=F32)
         gate_v[:, cols] = out[:HID].astype(BF16)
         up_v[:, cols] = out[HID:].astype(BF16)
         for i, (src, dst) in enumerate(((gate_v, grad_gate), (up_v, grad_up))):
@@ -414,7 +416,7 @@
         kernel,
         out_shape=(
             pltpu.VMEM((2 * HID, 512), BF16),
-            pltpu.VMEM((D, 512), BF16),
+            pltpu.VMEM((512, D), BF16),
             pltpu.VMEM((16, D), F32),
         ),
         in_specs=[hbm] * 7,

time: 70 us -> 68.7 us (0.981)
  Pallas kernels: 69.2 us -> 67.4 us
    pallas_call x1, Pallas kernels: 66.1 us -> 64.9 us  [body(): pl.pallas_call(kernel, out_shape=(pltpu.VMEM((2 * HID, 512), BF16), pltpu...]
where the time goes in v4:
time: 68.7 us; the launch traced here: 68 us
  Pallas kernels  67.4 us (98%)
    pallas_call x1, Pallas kernels, body(): pl.pallas_call(kernel, out_shape=(pltpu.VMEM((2 * HID, 512), BF16), pltpu...  64.9 us
    pallas_call x1, Pallas kernels, body(): pl.pallas_call(finish_kernel, out_shape=(jax.ShapeDtypeStruct((HID, D), B...  2.48 us

profile of v4, /device:TPU:6, one launch (start us, length us, event | category | flops | bytes accessed | tf_op | source)
XLA Modules:
  0.0 68.0 jit_solution(15031816942934278901)
XLA Ops:
  0.6 0.0 copy-start.1
  0.6 0.0 copy-start
  0.7 64.9 %gather_and_forward.1 = (bf16[176,512]{1,0:T(8,128)(2,1)S(1)}, bf16[512,4096]{1,0:T(8,128)(2,1)S(1)}, f32[16,4096]{1,0:T(8,128)S(1)}) custom-call(bf16[64,512]{1,0:T(8,128)(2,1)} %bitcast.15, bf16[64,512]{1,0:T(8,128)(2,1)} %bitcast.16, bf16[32,128]{1,0:T(8,128)(2,1)} %bitcast.17, bf16[88,4096]{1,0:T(8,128)(2,1)} %bitcast.9, bf16[88,4096]{1,0:T(8,128)(2,1)} %bitcast.10, ...), custom_call_target="tpu_custom_call" | custom-call | flops 1107296256 | bytes 8388608 | tf_op jit(solution)/shard_map/gather_and_forward/pallas_call | solution.py:415
  65.5 0.0 copy-done.1
  65.5 0.0 copy-done
  65.6 2.5 %gradients_and_outer_update.1 = (bf16[88,4096]{1,0:T(8,128)(2,1)}, bf16[88,4096]{1,0:T(8,128)(2,1)}, f32[11,4096]{1,0:T(8,128)}, bf16[11,4096]{1,0:T(8,128)(2,1)}) custom-call(bf16[176,512]{1,0:T(8,128)(2,1)S(1)} %get-tuple-element.11.d_ref, bf16[512,4096]{1,0:T(8,128)(2,1)S(1)} %get-tuple-element.12.normed_ref, f32[16,4096]{1,0:T(8,128)S(1)} %get-tuple-element.13.total_ref, ...), custom_call_target="tpu_custom_call" | custom-call | flops 738197504 | bytes 6291456 | tf_op jit(solution)/shard_map/gradients_and_outer_update/pallas_call | solution.py:469
Async XLA Ops:
  0.6 64.9 %copy-start.1 = (bf16[11,4096]{1,0:T(8,128)(2,1)S(1)}, bf16[11,4096]{1,0:T(8,128)(2,1)}, u32[]{:S(2)}) copy-start(bf16[11,4096]{1,0:T(8,128)(2,1)} %anchor_ref.1) | copy-start | bytes 270340
  0.6 64.9 %copy-start = (f32[11,4096]{1,0:T(8,128)S(1)}, f32[11,4096]{1,0:T(8,128)}, u32[]{:S(2)}) copy-start(f32[11,4096]{1,0:T(8,128)} %mom_ref.1) | copy-start | bytes 540676

commit v5 on v4

--- a/solution.py
+++ b/solution.py
@@ -19,18 +19,18 @@
 NT = (((1,), (1,)), ((), ()))
 NN = (((1,), (0,)), ((), ()))
 TOK, COT = 0, 1
+DIRECT = ((TOK, 0), (COT, 0))
 ORDER = (
-    ('F', 0, 0), ('Z', 0), ('S', 0, 0, 0), ('F', 1, 0), ('S', 1, 0, 0), ('FF', 0, 0), ('SF', 0, 0, 0),
-    ('FF', 1, 0), ('PG',), ('SF', 1, 0, 0), ('Z', 1), ('S', 0, 0, 1), ('S', 1, 0, 1), ('F', 0, 1),
-    ('F', 0, 3), ('ZF', 0), ('S', 0, 1, 0), ('SF', 0, 0, 1), ('OP',), ('SF', 1, 0, 1), ('FF', 0, 1),
-    ('S', 0, 3, 0), ('FF', 0, 3), ('ZF', 1), ('SF', 0, 1, 0), ('S', 1, 3, 0), ('F', 1, 3), ('F', 1, 1),
-    ('S', 0, 1, 1), ('PD',), ('OL',), ('SQ', 0, 0), ('F', 0, 2), ('S', 0, 2, 0), ('S', 0, 3, 1),
-    ('SF', 0, 1, 1), ('FF', 0, 2), ('F', 1, 2), ('S', 1, 1, 0), ('S', 1, 2, 0), ('SF', 0, 3, 0), ('FF', 1, 1),
-    ('SF', 0, 2, 0), ('FF', 1, 3), ('S', 0, 2, 1), ('FF', 1, 2), ('SF', 0, 3, 1), ('BW', 1, 0), ('PU',),
-    ('S', 1, 1, 1), ('SF', 0, 2, 1), ('S', 1, 3, 1), ('S', 1, 2, 1), ('SF', 1, 1, 0), ('SF', 1, 1, 1),
-    ('SQ', 0, 3), ('SQ', 0, 1), ('SQ', 0, 2), ('SF', 1, 2, 0), ('FW', 0), ('SF', 1, 3, 0), ('OF',),
-    ('SF', 1, 3, 1), ('FW', 1), ('SF', 1, 2, 1), ('FW', 2), ('FW', 3), ('BW', 1, 1), ('BW', 1, 3),
-    ('BW', 1, 2),
+    ('Z', 0), ('F', 0, 0), ('Z', 1), ('F', 1, 0), ('S', 0, 0, 0), ('S', 1, 0, 0), ('PG',), ('OP',),
+    ('S', 0, 0, 1), ('PU',), ('S', 1, 0, 1), ('SF', 1, 0, 0), ('SF', 0, 0, 0), ('ZF', 0), ('S', 0, 1, 0),
+    ('F', 0, 1), ('F', 0, 3), ('S', 0, 3, 0), ('SF', 1, 0, 1), ('SF', 0, 0, 1), ('FF', 0, 1), ('SF', 0, 1, 0),
+    ('FF', 0, 3), ('SF', 0, 3, 0), ('S', 1, 3, 0), ('ZF', 1), ('F', 1, 3), ('F', 1, 1), ('S', 0, 1, 1),
+    ('F', 0, 2), ('S', 1, 1, 0), ('S', 0, 3, 1), ('PD',), ('SQ', 0, 0), ('OL',), ('FF', 1, 3), ('FF', 1, 1),
+    ('FF', 0, 2), ('S', 0, 2, 0), ('F', 1, 2), ('SF', 0, 1, 1), ('SF', 0, 3, 1), ('BW', 1, 0), ('S', 0, 2, 1),
+    ('SF', 0, 2, 0), ('FF', 1, 2), ('S', 1, 2, 0), ('S', 1, 3, 1), ('SF', 0, 2, 1), ('S', 1, 1, 1),
+    ('S', 1, 2, 1), ('SQ', 0, 3), ('SF', 1, 3, 1), ('SQ', 0, 2), ('SQ', 0, 1), ('SF', 1, 3, 0),
+    ('SF', 1, 1, 0), ('SF', 1, 2, 0), ('FW', 0), ('SF', 1, 1, 1), ('FW', 1), ('SF', 1, 2, 1), ('OF',),
+    ('FW', 2), ('FW', 3), ('BW', 1, 3), ('BW', 1, 1), ('BW', 1, 2),
 )
 GROUPS = {
     (0, 0): ((0, 1), (1, 4)),
@@ -60,8 +60,8 @@
     def at(yy, xx, zz):
         return {"fsdp": ((yy + 4) % 4) * 16 + ((xx + 4) % 4) * 4 + (zz + 4) % 4}
 
-    xn = (at(y, x + 1, zh), at(y, x - 1, zh))
-    yn = (at(y + 1, x, zh), at(y - 1, x, zh))
+    xn = (at(y, x + 1, zh), at(y, x - 1, zh), at(y, x + 2, zh))
+    yn = (at(y + 1, x, zh), at(y - 1, x, zh), at(y + 2, x, zh))
     zn = (at(y, x, zh + 1), at(y, x, zh - 1))
     partner = {"rep": zl * 2 + 1 - core}
     line = [{"rep": ((zl + k) % 4) * 2 + core} for k in (1, 2, 3)]
@@ -121,8 +121,12 @@
             src = b.at[0, 0]
             xy(task, h, 0, src, b.at[0, 3], near(h)[0][0])
             xy(task, h, 1, src, b.at[0, 1], near(h)[0][1])
+            if task in DIRECT:
+                xy(task, h, 2, src, b.at[0, 2], near(h)[0][2])
 
     def first_forward(task):
+        if task in DIRECT:
+            return
         for h in range(2):
             b = g.at[task[0], h, task[1]]
             need((task, h, 0))
@@ -137,7 +141,7 @@
         for h in range(2):
             b = g.at[task[0], h, task[1]]
             for offset in range(first, last):
-                for k in brings[offset]:
+                for k in (2,) if task in DIRECT and offset == 2 else brings[offset]:
                     need((task, h, k))
             cols = pl.ds(first, last - first)
             src = b.at[0, cols]
@@ -284,7 +288,7 @@
         squares[...] = jnp.broadcast_to(1.0 / jnp.sqrt(total / D + norm_epsilon), squares.shape)
 
     def forward(first, last):
-        @pl.loop(first, last)
+        @pl.loop(first, last, unroll=2)
         def _(b):
             ry, rx = (b // 4 - y + 4) % 4, (b % 4 - x + 4) % 4
             cols = pl.ds(pl.multiple_of(b * 256, 256), 256)
@@ -305,7 +309,7 @@
         rz = task[1]
         zs = (zh + rz) % 4
 
-        @pl.loop(0, 4)
+        @pl.loop(0, 4, unroll=4)
         def _(yy):
             ry = (yy - y + 4) % 4
             rows = jnp.concatenate(

time: 68.7 us -> 68 us (0.990)
  Pallas kernels: 67.4 us -> 66.5 us
    pallas_call x1, Pallas kernels: 64.9 us -> 64 us  [body(): pl.pallas_call(kernel, out_shape=(pltpu.VMEM((2 * HID, 512), BF16), pltpu...]
where the time goes in v5:
time: 68 us; the launch traced here: 67.2 us
  Pallas kernels  66.5 us (98%)
    pallas_call x1, Pallas kernels, body(): pl.pallas_call(kernel, out_shape=(pltpu.VMEM((2 * HID, 512), BF16), pltpu...  64 us
    pallas_call x1, Pallas kernels, body(): pl.pallas_call(finish_kernel, out_shape=(jax.ShapeDtypeStruct((HID, D), B...  2.49 us

profile of v5, /device:TPU:6, one launch (start us, length us, event | category | flops | bytes accessed | tf_op | source)
XLA Modules:
  0.0 67.2 jit_solution(14835890907638710151)
XLA Ops:
  0.6 0.0 copy-start.1
  0.6 0.0 copy-start
  0.7 64.0 %gather_and_forward.1 = (bf16[176,512]{1,0:T(8,128)(2,1)S(1)}, bf16[512,4096]{1,0:T(8,128)(2,1)S(1)}, f32[16,4096]{1,0:T(8,128)S(1)}) custom-call(bf16[64,512]{1,0:T(8,128)(2,1)} %bitcast.15, bf16[64,512]{1,0:T(8,128)(2,1)} %bitcast.16, bf16[32,128]{1,0:T(8,128)(2,1)} %bitcast.17, bf16[88,4096]{1,0:T(8,128)(2,1)} %bitcast.9, bf16[88,4096]{1,0:T(8,128)(2,1)} %bitcast.10, ...), custom_call_target="tpu_custom_call" | custom-call | flops 1107296256 | bytes 8388608 | tf_op jit(solution)/shard_map/gather_and_forward/pallas_call | solution.py:419
  64.6 0.0 copy-done.1
  64.7 0.0 copy-done
  64.7 2.5 %gradients_and_outer_update.1 = (bf16[88,4096]{1,0:T(8,128)(2,1)}, bf16[88,4096]{1,0:T(8,128)(2,1)}, f32[11,4096]{1,0:T(8,128)}, bf16[11,4096]{1,0:T(8,128)(2,1)}) custom-call(bf16[176,512]{1,0:T(8,128)(2,1)S(1)} %get-tuple-element.11.d_ref, bf16[512,4096]{1,0:T(8,128)(2,1)S(1)} %get-tuple-element.12.normed_ref, f32[16,4096]{1,0:T(8,128)S(1)} %get-tuple-element.13.total_ref, ...), custom_call_target="tpu_custom_call" | custom-call | flops 738197504 | bytes 6291456 | tf_op jit(solution)/shard_map/gradients_and_outer_update/pallas_call | solution.py:473
Async XLA Ops:
  0.6 64.0 %copy-start.1 = (bf16[11,4096]{1,0:T(8,128)(2,1)S(1)}, bf16[11,4096]{1,0:T(8,128)(2,1)}, u32[]{:S(2)}) copy-start(bf16[11,4096]{1,0:T(8,128)(2,1)} %anchor_ref.1) | copy-start | bytes 270340
  0.6 64.0 %copy-start = (f32[11,4096]{1,0:T(8,128)S(1)}, f32[11,4096]{1,0:T(8,128)}, u32[]{:S(2)}) copy-start(f32[11,4096]{1,0:T(8,128)} %mom_ref.1) | copy-start | bytes 540676

commit v6 on v5

--- a/solution.py
+++ b/solution.py
@@ -274,7 +274,7 @@
     def add_squares(task):
         arrive(task)
 
-        @pl.loop(0, 16)
+        @pl.loop(0, 16, unroll=2)
         def _(b):
             v = block_of(TOK, task[1], b // 4, b % 4).astype(F32)
             v = v * v

time: 68 us -> 68 us (level)
  no operation moved by 1% of the time
where the time goes in v6:
time: 68 us; the launch traced here: 67.2 us
  Pallas kernels  66.5 us (98%)
    pallas_call x1, Pallas kernels, body(): pl.pallas_call(kernel, out_shape=(pltpu.VMEM((2 * HID, 512), BF16), pltpu...  64 us
    pallas_call x1, Pallas kernels, body(): pl.pallas_call(finish_kernel, out_shape=(jax.ShapeDtypeStruct((HID, D), B...  2.49 us

profile of v6, /device:TPU:6, one launch (start us, length us, event | category | flops | bytes accessed | tf_op | source)
XLA Modules:
  0.0 67.2 jit_solution(11014763952963718745)
XLA Ops:
  0.6 0.0 copy-start.1
  0.6 0.0 copy-start
  0.7 64.0 %gather_and_forward.1 = (bf16[176,512]{1,0:T(8,128)(2,1)S(1)}, bf16[512,4096]{1,0:T(8,128)(2,1)S(1)}, f32[16,4096]{1,0:T(8,128)S(1)}) custom-call(bf16[64,512]{1,0:T(8,128)(2,1)} %bitcast.15, bf16[64,512]{1,0:T(8,128)(2,1)} %bitcast.16, bf16[32,128]{1,0:T(8,128)(2,1)} %bitcast.17, bf16[88,4096]{1,0:T(8,128)(2,1)} %bitcast.9, bf16[88,4096]{1,0:T(8,128)(2,1)} %bitcast.10, ...), custom_call_target="tpu_custom_call" | custom-call | flops 1107296256 | bytes 8388608 | tf_op jit(solution)/shard_map/gather_and_forward/pallas_call | solution.py:419
  64.6 0.0 copy-done.1
  64.7 0.0 copy-done
  64.7 2.5 %gradients_and_outer_update.1 = (bf16[88,4096]{1,0:T(8,128)(2,1)}, bf16[88,4096]{1,0:T(8,128)(2,1)}, f32[11,4096]{1,0:T(8,128)}, bf16[11,4096]{1,0:T(8,128)(2,1)}) custom-call(bf16[176,512]{1,0:T(8,128)(2,1)S(1)} %get-tuple-element.11.d_ref, bf16[512,4096]{1,0:T(8,128)(2,1)S(1)} %get-tuple-element.12.normed_ref, f32[16,4096]{1,0:T(8,128)S(1)} %get-tuple-element.13.total_ref, ...), custom_call_target="tpu_custom_call" | custom-call | flops 738197504 | bytes 6291456 | tf_op jit(solution)/shard_map/gradients_and_outer_update/pallas_call | solution.py:473
Async XLA Ops:
  0.6 64.0 %copy-start.1 = (bf16[11,4096]{1,0:T(8,128)(2,1)S(1)}, bf16[11,4096]{1,0:T(8,128)(2,1)}, u32[]{:S(2)}) copy-start(bf16[11,4096]{1,0:T(8,128)(2,1)} %anchor_ref.1) | copy-start | bytes 270340
  0.6 64.0 %copy-start = (f32[11,4096]{1,0:T(8,128)S(1)}, f32[11,4096]{1,0:T(8,128)}, u32[]{:S(2)}) copy-start(f32[11,4096]{1,0:T(8,128)} %mom_ref.1) | copy-start | bytes 540676
